TPU v7x, 128 devices: a whole 4x4x4 slice. The times are simulated.
128 devices in a mesh: row: 16 (over z_hi, y, core), col: 8 (over z_lo, x).
Axes of the slice: x: 4, y: 4, z: 4 (z_hi: 2, z_lo: 2; z = z_hi * 2 + z_lo), core: 2. Of those that a mesh axis runs over, the one named last changes fastest.
Arguments:
- node_features: bfloat16 [32768, 128], P(('row', 'col')), may hold values from -6 to 6
- tile_values: bfloat16 [16, 8, 384, 128, 128], P('row', 'col'), may hold values from -0.109375 to 0.109375
- tile_rows: int32 [16, 8, 384], P('row', 'col'), may hold values from 0 to 15
- tile_cols: int32 [16, 8, 384], P('row', 'col'), may hold values from 0 to 31
- tile_count: int32 [16, 8], P('row', 'col'), may hold values from 48 to 384, as said below
- labels: int32 [32768], P(('row', 'col')), may hold values from 0 to 46
- train_mask: int32 [32768], P(('row', 'col')), may hold values from 0 to 1, as said below
- hidden_weight: bfloat16 [128, 256], replicated, may hold values from -0.5 to 0.5
- hidden_bias: float32 [256], replicated, may hold values from -3 to 3
- class_weight: bfloat16 [256, 47], replicated, may hold values from -3.59375 to 3.59375
- class_bias: float32 [47], replicated, may hold values from -4 to 4
Outputs:
- hidden: bfloat16 [32768, 256], P(('row', 'col'))
- logits: float32 [47, 32768], P(None, ('row', 'col'))
- mean_loss: float32 [], replicated
- hidden_weight_grad: float32 [128, 256], replicated
- hidden_bias_grad: float32 [256], replicated
- class_weight_grad: float32 [256, 47], replicated
- class_bias_grad: float32 [47], replicated
Inputs may be any that keep to these rules, and one draw needn't show every extreme that they name: Slots s >= tile_count of a block are not part of it; some block has all 384 slots live. `train_mask`: at least one node is a training node.
All inputs are finite; a program needn't handle non-finite values.
Results may differ from a plain program's by a relative error of at most 0.025.
Values may be sent and summed in bfloat16 or wider, within the bound.
A program may use at most 128 MiB of HBM per device.

v0:
```python
import math

import jax
import jax.numpy as jnp
from jax import lax
from jax.sharding import PartitionSpec as P


def tile_product(values, source_tile, target_tile, live_slots, source, out_tiles, transpose):
    feature_width = source.shape[1]
    wide_source = source.dtype == jnp.float32
    tiled = source.reshape(-1, 128, feature_width)
    slot_count = values.shape[0]
    group_size = math.gcd(slot_count, 32)
    rounds = slot_count // group_size
    grouped = (
        values.reshape(rounds, group_size, 128, 128),
        source_tile.reshape(rounds, group_size),
        target_tile.reshape(rounds, group_size),
        live_slots.reshape(rounds, group_size),
    )
    pattern = "gji,gjf->gif" if transpose else "gij,gjf->gif"
    targets = jnp.arange(out_tiles, dtype=jnp.int32)

    def one_group(totals, item):
        tiles_in, from_tile, to_tile, alive = item
        pieces = tiled[from_tile]
        if wide_source:
            product = jnp.einsum(
                pattern, tiles_in.astype(jnp.float32), pieces, precision=lax.Precision.HIGHEST
            )
        else:
            product = jnp.einsum(pattern, tiles_in, pieces, preferred_element_type=jnp.float32)
        placing = (targets[:, None] == to_tile[None, :]).astype(jnp.float32) * alive[None, :]
        placed = jnp.einsum("og,gif->oif", placing, product, precision=lax.Precision.HIGHEST)
        return (totals + placed, None)

    start = jnp.zeros((out_tiles, 128, feature_width), jnp.float32)
    totals, _ = lax.scan(one_group, start, grouped)
    return totals.reshape(out_tiles * 128, feature_width)


def pre_activation(aggregated, hidden_weight, hidden_bias):
    return jnp.dot(aggregated, hidden_weight, preferred_element_type=jnp.float32) + hidden_bias


def on_device(
    node_features,
    tile_values,
    tile_rows,
    tile_cols,
    tile_count,
    labels,
    train_mask,
    hidden_weight,
    hidden_bias,
    class_weight,
    class_bias,
):
    nodes_here = node_features.shape[0]
    values = tile_values[0, 0]
    rows_here = tile_rows[0, 0]
    cols_here = tile_cols[0, 0]
    live_slots = (jnp.arange(values.shape[0]) < tile_count[0, 0]).astype(jnp.float32)
    block_rows = lax.axis_size("col") * nodes_here // 128
    block_cols = lax.axis_size("row") * nodes_here // 128
    class_weight_wide = class_weight.astype(jnp.float32)
    gathered = lax.all_gather(node_features, "row", axis=0, tiled=True)
    first_term = tile_product(values, cols_here, rows_here, live_slots, gathered, block_rows, False)
    first_agg = lax.psum_scatter(
        first_term.astype(jnp.bfloat16), "col", scatter_dimension=0, tiled=True
    )
    hidden_pre = pre_activation(first_agg, hidden_weight, hidden_bias)
    hidden = jax.nn.silu(hidden_pre).astype(jnp.bfloat16)
    hidden_column = lax.all_gather(hidden, "row", axis=0, tiled=True)
    second_term = tile_product(
        values, cols_here, rows_here, live_slots, hidden_column, block_rows, False
    )
    second_agg = lax.psum_scatter(
        second_term.astype(jnp.bfloat16), "col", scatter_dimension=0, tiled=True
    ).astype(jnp.float32)
    logits = (
        jnp.einsum("hk,nh->kn", class_weight_wide, second_agg, precision=lax.Precision.HIGHEST)
        + class_bias[:, None]
    )
    top = jnp.max(logits, axis=0)
    log_total = top + jnp.log(jnp.sum(jnp.exp(logits - top[None, :]), axis=0))
    onehot = (jnp.arange(logits.shape[0])[:, None] == labels[None, :]).astype(jnp.float32)
    cross_entropy = log_total - jnp.sum(onehot * logits, axis=0)
    weights = train_mask.astype(jnp.float32)
    count, loss_total = lax.psum(
        (jnp.sum(weights), jnp.sum(weights * cross_entropy)), ("row", "col")
    )
    mean_loss = loss_total / count
    class_grad = (jnp.exp(logits - log_total[None, :]) - onehot) * (weights / count)[None, :]
    class_bias_part = jnp.sum(class_grad, axis=1)
    class_weight_part = jnp.einsum(
        "nh,kn->hk", second_agg, class_grad, precision=lax.Precision.HIGHEST
    )
    agg_grad = jnp.einsum(
        "kn,hk->nh", class_grad, class_weight_wide, precision=lax.Precision.HIGHEST
    )
    grad_block = lax.all_gather(agg_grad.astype(jnp.bfloat16), "col", axis=0, tiled=True).astype(
        agg_grad.dtype
    )
    back_term = tile_product(values, rows_here, cols_here, live_slots, grad_block, block_cols, True)
    hidden_grad = lax.psum_scatter(
        back_term.astype(jnp.bfloat16), "row", scatter_dimension=0, tiled=True
    ).astype(jnp.float32)
    sigma = jax.nn.sigmoid(hidden_pre)
    pre_grad = hidden_grad * sigma * (1.0 + hidden_pre * (1.0 - sigma))
    hidden_weight_part = jnp.einsum(
        "nf,nh->fh", first_agg.astype(jnp.float32), pre_grad, precision=lax.Precision.HIGHEST
    )
    hidden_bias_part = jnp.sum(pre_grad, axis=0)
    hidden_weight_grad, hidden_bias_grad, class_weight_grad, class_bias_grad = lax.psum(
        (hidden_weight_part, hidden_bias_part, class_weight_part, class_bias_part), ("row", "col")
    )
    return (
        hidden,
        logits,
        mean_loss,
        hidden_weight_grad,
        hidden_bias_grad,
        class_weight_grad,
        class_bias_grad,
    )


def solution(mesh):
    in_specs = (
        P(("row", "col"), None),
        P("row", "col", None, None, None),
        P("row", "col", None),
        P("row", "col", None),
        P("row", "col"),
        P(("row", "col")),
        P(("row", "col")),
        P(),
        P(),
        P(),
        P(),
    )
    out_specs = (P(("row", "col"), None), P(None, ("row", "col")), P(), P(), P(), P(), P())
    return jax.shard_map(
        on_device, mesh=mesh, in_specs=in_specs, out_specs=out_specs, check_vma=False
    )
```

profile of v0, /device:TPU:1, one launch (start us, length us, event | category | flops | bytes accessed | tf_op | source)
XLA Modules:
  0.0 891.0 jit_solution(12447308209618001124)
XLA Ops:
  10.2 49.1 %all-gather.4.cloned.1.call-done = bf16[4096,128]{1,0:T(8,128)(2,1)} async-done(((bf16[256,128]{1,0:T(8,128)(2,1)}), bf16[4096,128]{1,0:T(8,128)(2,1)}) %all-gather.4.cloned.1.call-update) | async-done | bytes 1048592 | tf_op jit(solution)/shard_map/all_gather | solution.py:68
  59.3 76.7 %while.33 = (s32[]{:T(128)}, f32[16,128,128]{2,0,1:T(8,128)S(1)}, s32[12,32]{1,0:T(8,128)S(1)}, f32[12,32]{1,0:T(8,128)S(1)}, bf16[12,32,128,128]{3,2,1,0:T(8,12...) while((s32[]{:T(128)}, f32[16,128,128]{2,0,1:T(8,128)S(1)}, ...), condition=%wide.region_1.2_spmd.clone, body=%wide.region_0.1_spmd.clone.sunk | while | flops 235407456 | bytes 10491263 | solution.py:39
  137.2 31.0 %reduce-scatter.4.cloned.1.call-done = bf16[256,128]{1,0:T(8,128)(2,1)} async-done(((bf16[2048,128]{1,0:T(8,128)(2,1)}), bf16[256,128]{1,0:T(8,128)(2,1)}) %reduce-scatter.4.cloned.1.call-update) | async-done | bytes 65552 | tf_op jit(solution)/shard_map/reduce_scatter | solution.py:70
  170.2 54.0 %all-gather.6.cloned.1.call-done = bf16[4096,256]{1,0:T(8,128)(2,1)} async-done(((bf16[256,256]{1,0:T(8,128)(2,1)}), bf16[4096,256]{1,0:T(8,128)(2,1)}) %all-gather.6.cloned.1.call-update) | async-done | bytes 2097168 | tf_op jit(solution)/shard_map/all_gather | solution.py:75
  224.2 133.6 %while.34 = (s32[]{:T(128)}, f32[16,128,256]{2,0,1:T(8,128)}, s32[12,32]{1,0:T(8,128)S(1)}, f32[12,32]{1,0:T(8,128)S(1)}, bf16[12,32,128,128]{3,2,1,0:T(8,128)(2...) while((s32[]{:T(128)}, f32[16,128,256]{2,0,1:T(8,128)}, ...), condition=%wide.region_4.5_spmd.clone, body=%wide.region_3.4_spmd.clone.sunk | while | flops 470812768 | bytes 36705716 | solution.py:39
  228.7 5.4 select_add_fusion.4
  362.3 64.9 %psum.43 = f32[]{:T(128)} all-reduce(f32[]{:T(128)} %convert_reduce_fusion), channel_id=1, replica_groups=mesh['row'=16,'col'=8] {'row','col'}, use_global_device_ids=true, to_apply=%region_12.13 | all-reduce | flops 1 | bytes 8 | tf_op jit(solution)/shard_map/psum | solution.py:91
  430.4 30.7 %all-gather.8.cloned.1.call-done = bf16[2048,256]{1,0:T(8,128)(2,1)} async-done(((bf16[256,256]{1,0:T(8,128)(2,1)}), bf16[2048,256]{1,0:T(8,128)(2,1)}) %all-gather.8.cloned.1.call-update) | async-done | bytes 1048592 | tf_op jit(solution)/shard_map/all_gather | solution.py:103
  462.6 193.6 %while.35 = (s32[]{:T(128)}, f32[32,128,256]{2,0,1:T(8,128)}, s32[12,32]{1,0:T(8,128)S(1)}, f32[12,32]{1,0:T(8,128)S(1)}, bf16[12,32,128,128]{3,2,1,0:T(8,128)(2...) while((s32[]{:T(128)}, f32[32,128,256]{2,0,1:T(8,128)}, ...), condition=%wide.region_14.15_spmd.clone, body=%wide.region_13.14_spmd.clone.sunk | while | flops 2015366272 | bytes 63968692 | solution.py:39
  470.5 6.3 select_add_fusion.5
  486.6 6.3 select_add_fusion.5
  502.7 6.3 select_add_fusion.5
  518.9 6.3 select_add_fusion.5
  535.0 6.3 select_add_fusion.5
  551.1 6.3 select_add_fusion.5
  567.2 6.3 select_add_fusion.5
  583.4 6.3 select_add_fusion.5
  599.5 6.3 select_add_fusion.5
  615.6 6.3 select_add_fusion.5
  631.8 6.3 select_add_fusion.5
  647.9 6.3 select_add_fusion.5
  661.6 72.9 %reduce-scatter.8.cloned.1.call-done = bf16[256,256]{1,0:T(8,128)(2,1)} async-done(((bf16[4096,256]{1,0:T(8,128)(2,1)}), bf16[256,256]{1,0:T(8,128)(2,1)}) %reduce-scatter.8.cloned.1.call-update) | async-done | bytes 131088 | tf_op jit(solution)/shard_map/reduce_scatter | solution.py:107
  737.1 66.4 %all-reduce = (f32[]{:T(128)}, f32[256]{0:T(256)}, f32[256,47]{0,1:T(8,128)}, f32[47]{0:T(128)}) all-reduce(f32[]{:T(128)} %multiply_reduce_fusion, f32[256]{0:T(256)S(1)} %get-tuple-element.262, f32[256,47]{0,1:T(8,128)S(1)} %fusion.62, f32[47]{0:T(128)S(1)} %get-tuple-element.214), channel_id=1, replica_groups=mesh['row'=16,'col'=8] {'row','col'}, use_global_device_ids=true, to_apply=%region_10.11 | all-reduce | flops 12336 | bytes 98688 | tf_op jit(solution)/shard_map/psum | solution.py:91
  804.8 76.8 %all-reduce.3.cloned.1.call-done = f32[128,256]{1,0:T(8,128)} async-done(((f32[128,256]{1,0:T(8,128)}), f32[128,256]{1,0:T(8,128)}) %all-reduce.3.cloned.1.call-update) | async-done | bytes 131088 | tf_op jit(solution)/shard_map/psum | solution.py:116
  (394 shorter events, 344.5 us)
Async XLA Ops:
  7.2 161.0 %copy-start = (bf16[128,256]{1,0:T(8,128)(2,1)S(1)}, bf16[128,256]{1,0:T(8,128)(2,1)}, u32[]{:S(2)}) copy-start(bf16[128,256]{1,0:T(8,128)(2,1)} %param.24) | copy-start | bytes 196612
  7.2 52.1 %all-gather.4.cloned.1.call-start = ((), (), s32[]{:S(2)}) async-start(), calls=%async_computation.3 | async-start | bytes 1114112 | tf_op jit(solution)/shard_map/all_gather | solution.py:68
  7.9 160.3 %reduce-scatter.4.cloned.1.call-start = ((), (), s32[]{:S(2)}) async-start(), calls=%async_computation.4 | async-start | bytes 589824 | tf_op jit(solution)/shard_map/reduce_scatter | solution.py:70
  59.3 108.9 %copy-start.12 = (f32[256]{0:T(256)S(1)}, f32[256]{0:T(256)}, u32[]{:S(2)}) copy-start(f32[256]{0:T(256)} %param.25) | copy-start | bytes 3076
  137.1 87.1 %all-gather.6.cloned.1.call-start = ((), (), s32[]{:S(2)}) async-start(), calls=%async_computation.5 | async-start | bytes 2228224 | tf_op jit(solution)/shard_map/all_gather | solution.py:75
  169.9 257.9 %reduce-scatter.6.cloned.1.call-start = ((), (), s32[]{:S(2)}) async-start(), calls=%async_computation.6 | async-start | bytes 1179648 | tf_op jit(solution)/shard_map/reduce_scatter | solution.py:79
  357.8 70.1 %copy-start.7 = (bf16[256,47]{0,1:T(8,128)(2,1)S(1)}, bf16[256,47]{0,1:T(8,128)(2,1)}, u32[]{:S(2)}) copy-start(bf16[256,47]{0,1:T(8,128)(2,1)} %param.26) | copy-start | bytes 72196
  357.8 70.1 %copy-start.11 = (f32[47]{0:T(128)S(1)}, f32[47]{0:T(128)}, u32[]{:S(2)}) copy-start(f32[47]{0:T(128)} %param.27) | copy-start | bytes 568
  357.8 71.2 %copy-start.9 = (s32[256]{0:T(256)S(1)}, s32[256]{0:T(256)}, u32[]{:S(2)}) copy-start(s32[256]{0:T(256)} %param.22) | copy-start | bytes 3076
  361.6 99.5 %all-gather.8.cloned.1.call-start = ((), (), s32[]{:S(2)}) async-start(), calls=%async_computation.7 | async-start | bytes 1179648 | tf_op jit(solution)/shard_map/all_gather | solution.py:103
  429.0 232.4 %copy-start.5 = (f32[256,47]{0,1:T(8,128)}, f32[256,47]{0,1:T(8,128)S(1)}, u32[]{:S(2)}) copy-start(f32[256,47]{0,1:T(8,128)S(1)} %get-tuple-element.267) | copy-start | bytes 144388
  430.1 304.4 %reduce-scatter.8.cloned.1.call-start = ((), (), s32[]{:S(2)}) async-start(), calls=%async_computation.8 | async-start | bytes 2228224 | tf_op jit(solution)/shard_map/reduce_scatter | solution.py:107
  465.4 5.0 copy-start.1
  481.6 5.0 copy-start.1
  497.7 5.0 copy-start.1
  513.8 5.0 copy-start.1
  529.9 5.0 copy-start.1
  546.1 5.0 copy-start.1
  578.3 5.0 copy-start.1
  594.5 5.0 copy-start.1
  626.7 5.0 copy-start.1
  642.8 5.0 copy-start.1
  658.7 76.9 %copy-start.8 = (bf16[256,128]{1,0:T(8,128)(2,1)S(1)}, bf16[256,128]{1,0:T(8,128)(2,1)}, u32[]{:S(2)}) copy-start(bf16[256,128]{1,0:T(8,128)(2,1)} %reduce-scatter.4.cloned.1.call-done) | copy-start | bytes 196612
  661.2 220.3 %all-reduce.3.cloned.1.call-start = ((), (), s32[]{:S(2)}) async-start(), calls=%async_computation.9 | async-start | bytes 262144 | tf_op jit(solution)/shard_map/psum | solution.py:116
  (40 other events, 80.3 us)
Sparse Core Ops, SparseCore 0:
  10.5 48.7 all-gather.3
  137.3 30.8 reduce-scatter.3
  171.5 52.6 all-gather.5
  361.7 32.5 reduce-scatter.5
  430.2 30.8 all-gather.7
  661.4 73.1 reduce-scatter.7
  740.6 140.8 all-reduce.2
where the time goes:
time: 893 us; the launch traced here: 891 us
  waiting for transfers between devices  315 us (35%)
  matrix products  282 us (32%)
  local copies, waits for them, and re-layouts  133 us (15%)
  blocking collectives  131 us (15%)
  between operations  17.3 us (2%)
  other arithmetic  8.93 us (1%)
    dot_general x36, matrix products, one_group(): jnp.einsum('og,gif->oif', placing, product, precision=lax.Precision.HIGHEST)  173 us
    psum x2, blocking collectives, on_device(): lax.psum((jnp.sum(weights), jnp.sum(weights * cross_entropy)), ('row', 'c...  131 us
    gather x36, local copies, waits for them, and re-layouts, one_group(): pieces = tiled[from_tile]  84.4 us
    psum x1, waiting for transfers between devices, on_device(): lax.psum((hidden_weight_part, hidden_bias_part, class_weight_part, class_...  76.8 us
    reduce_scatter x1, waiting for transfers between devices, on_device(): lax.psum_scatter(back_term.astype(jnp.bfloat16), 'row', scatter_dimension...  72.9 us
    dot_general x12, matrix products, one_group(): jnp.einsum(pattern, tiles_in.astype(jnp.float32), pieces, precision=lax.P...  60.3 us
    all_gather x1, waiting for transfers between devices, on_device(): hidden_column = lax.all_gather(hidden, 'row', axis=0, tiled=True)  54 us
    all_gather x1, waiting for transfers between devices, on_device(): gathered = lax.all_gather(node_features, 'row', axis=0, tiled=True)  49.1 us
  transfers between devices with their start and end apart: 7, of which 6 were waited for; matrix products, arithmetic and copies ran while one was open for 0% of the time, Pallas kernels for 0%

commit v1 on v0

v1 whole, which is shorter than its diff:
```python
import jax
import jax.numpy as jnp
from jax import lax
from jax.experimental import pallas as pl
from jax.experimental.pallas import tpu as pltpu
from jax.sharding import PartitionSpec as P

TILE = 128
PADDED = 48
NT = (((1,), (1,)), ((), ()))
TN = (((0,), (0,)), ((), ()))


def densify_kernel(n_rows, rows, cols, count, values, out, head, nxt, dups, sem):
    slots = values.shape[0]
    places = out.shape[0] - slots
    live = count[0, 0]
    zero = jnp.zeros((TILE, TILE), jnp.bfloat16)

    def clear(p, _):
        head[p] = -1
        out[p] = zero
        return 0

    lax.fori_loop(0, places, clear, 0, unroll=8)

    def place(s, found):
        p = cols[s] * n_rows + rows[s]
        alive = s < live
        before = head[p]
        first = jnp.logical_and(alive, before < 0)
        again = jnp.logical_and(alive, before >= 0)
        head[p] = jnp.where(alive, s, before)
        nxt[s] = before
        dups[found] = p
        pltpu.make_async_copy(
            values.at[s], out.at[jnp.where(first, p, places + s)], sem
        ).start()
        return found + again.astype(jnp.int32)

    found = lax.fori_loop(0, slots, place, 0, unroll=8)
    pltpu.make_async_copy(values, out.at[pl.ds(places, slots)], sem).wait()

    def merge(i, _):
        p = dups[i]
        top = head[p]

        @pl.when(top >= 0)
        def _():
            head[p] = -1

            def more(state):
                return nxt[state[0]] >= 0

            def add(state):
                s, total = state
                return nxt[s], total + out[places + s].astype(jnp.float32)

            _, total = lax.while_loop(more, add, (top, out[p].astype(jnp.float32)))
            out[p] = total.astype(jnp.bfloat16)

        return 0

    lax.fori_loop(0, found, merge, 0)


def densify(rows, cols, count, values, n_rows, n_cols):
    slots = values.shape[0]
    places = n_rows * n_cols
    smem = pl.BlockSpec(memory_space=pltpu.SMEM)
    return pl.pallas_call(
        lambda *refs: densify_kernel(n_rows, *refs),
        out_shape=pltpu.VMEM((places + slots, TILE, TILE), jnp.bfloat16),
        in_specs=[smem, smem, smem, pl.BlockSpec(memory_space=pltpu.HBM)],
        out_specs=pl.BlockSpec(memory_space=pltpu.VMEM),
        scratch_shapes=[
            pltpu.SMEM((places,), jnp.int32),
            pltpu.SMEM((slots,), jnp.int32),
            pltpu.SMEM((slots + 1,), jnp.int32),
            pltpu.SemaphoreType.DMA,
        ],
        compiler_params=pltpu.CompilerParams(vmem_limit_bytes=4 * 2**20),
        name="densify",
    )(rows, cols, count, values)


def square(dense, row_chunk, col_chunk, n_rows):
    halves = [
        dense[pl.ds((2 * col_chunk + h) * n_rows + 2 * row_chunk, 2)].reshape(2 * TILE, TILE)
        for h in range(2)
    ]
    return jnp.concatenate(halves, axis=1)


def first_kernel(n_rows, dense, source, out):
    def one_chunk(i, _):
        total = jnp.zeros((2 * TILE, source.shape[1]), jnp.float32)
        for k in range(source.shape[0] // (2 * TILE)):
            piece = source[k * 2 * TILE : (k + 1) * 2 * TILE, :]
            total += jnp.dot(
                square(dense, i, k, n_rows), piece, preferred_element_type=jnp.float32
            )
        out[pl.ds(i * 2 * TILE, 2 * TILE), :] = total.astype(out.dtype)
        return 0

    lax.fori_loop(0, n_rows // 2, one_chunk, 0)


def second_kernel(n_rows, dense, source, out):
    def one_chunk(i, _):
        total = jnp.zeros(out.shape[1:], jnp.float32)
        for k in range(source.shape[0]):
            total += lax.dot_general(
                source[k], square(dense, i, k, n_rows), NT, preferred_element_type=jnp.float32
            )
        out[i] = total.astype(out.dtype)
        return 0

    lax.fori_loop(0, n_rows // 2, one_chunk, 0)


def back_kernel(n_rows, dense, source, out):
    def one_chunk(k, _):
        total = jnp.zeros(out.shape[1:], jnp.float32)
        for i in range(source.shape[0]):
            total += jnp.dot(
                source[i], square(dense, i, k, n_rows), preferred_element_type=jnp.float32
            )
        out[k] = total.astype(out.dtype)
        return 0

    lax.fori_loop(0, out.shape[0], one_chunk, 0)


def on_dense(kernel, n_rows, dense, source, shape, name):
    vmem = pl.BlockSpec(memory_space=pltpu.VMEM)
    return pl.pallas_call(
        lambda *refs: kernel(n_rows, *refs),
        out_shape=jax.ShapeDtypeStruct(shape, jnp.bfloat16),
        in_specs=[vmem, vmem],
        out_specs=vmem,
        compiler_params=pltpu.CompilerParams(vmem_limit_bytes=12 * 2**20),
        name=name,
    )(pltpu.with_memory_space_constraint(dense, pltpu.VMEM), source)


def on_device(
    node_features,
    tile_values,
    tile_rows,
    tile_cols,
    tile_count,
    labels,
    train_mask,
    hidden_weight,
    hidden_bias,
    class_weight,
    class_bias,
):
    nodes = node_features.shape[0]
    classes = class_bias.shape[0]
    row_size, col_size = lax.axis_size("row"), lax.axis_size("col")
    n_rows, n_cols = col_size * nodes // TILE, row_size * nodes // TILE
    dense = densify(tile_rows[0, 0], tile_cols[0, 0], tile_count, tile_values[0, 0], n_rows, n_cols)
    gathered = lax.all_gather(node_features, "row", axis=0, tiled=True)
    first_term = on_dense(
        first_kernel, n_rows, dense, gathered, (n_rows * TILE, gathered.shape[1]), "first"
    )
    first_agg = lax.psum_scatter(first_term, "col", scatter_dimension=0, tiled=True)
    hidden_pre = (
        jnp.dot(first_agg, hidden_weight, preferred_element_type=jnp.float32) + hidden_bias
    )
    hidden = jax.nn.silu(hidden_pre).astype(jnp.bfloat16)
    weight = jnp.pad(class_weight, ((0, 0), (0, PADDED - classes)))
    score_part = lax.dot_general(
        weight, hidden, (((0,), (1,)), ((), ())), preferred_element_type=jnp.float32
    ).astype(jnp.bfloat16)
    parts = lax.all_gather(score_part, "row", axis=0)
    second_term = on_dense(second_kernel, n_rows, dense, parts, (col_size, PADDED, nodes), "second")
    scores = lax.psum_scatter(second_term, "col", scatter_dimension=0)
    logits = scores[:classes].astype(jnp.float32) + class_bias[:, None]
    top = jnp.max(logits, axis=0)
    log_total = top + jnp.log(jnp.sum(jnp.exp(logits - top[None, :]), axis=0))
    onehot = (jnp.arange(classes)[:, None] == labels[None, :]).astype(jnp.float32)
    cross_entropy = log_total - jnp.sum(onehot * logits, axis=0)
    weights = train_mask.astype(jnp.float32)
    class_grad = (jnp.exp(logits - log_total[None, :]) - onehot) * weights[None, :]
    grad = jnp.pad(class_grad, ((0, PADDED - classes), (0, 0))).astype(jnp.bfloat16)
    grads = lax.all_gather(grad, "col", axis=0)
    back_term = on_dense(back_kernel, n_rows, dense, grads, (row_size, PADDED, nodes), "back")
    back = lax.psum_scatter(back_term, "row", scatter_dimension=0)
    hidden_grad = lax.dot_general(
        back, weight, (((0,), (1,)), ((), ())), preferred_element_type=jnp.float32
    )
    sigma = jax.nn.sigmoid(hidden_pre)
    pre_grad = hidden_grad * sigma * (1.0 + hidden_pre * (1.0 - sigma))
    hidden_weight_part = lax.dot_general(
        first_agg, pre_grad.astype(jnp.bfloat16), TN, preferred_element_type=jnp.float32
    )
    class_weight_part = lax.dot_general(
        hidden, back[:classes], TN_CLASS, preferred_element_type=jnp.float32
    )
    sums = lax.psum(
        (
            hidden_weight_part,
            jnp.sum(pre_grad, axis=0),
            class_weight_part,
            jnp.sum(class_grad, axis=1),
            jnp.sum(weights * cross_entropy),
            jnp.sum(weights),
        ),
        ("row", "col"),
    )
    count = sums[5]
    return (
        hidden,
        logits,
        sums[4] / count,
        sums[0] / count,
        sums[1] / count,
        sums[2] / count,
        sums[3] / count,
    )


TN_CLASS = (((0,), (1,)), ((), ()))


def solution(mesh):
    in_specs = (
        P(("row", "col"), None),
        P("row", "col", None, None, None),
        P("row", "col", None),
        P("row", "col", None),
        P("row", "col"),
        P(("row", "col")),
        P(("row", "col")),
        P(),
        P(),
        P(),
        P(),
    )
    out_specs = (P(("row", "col"), None), P(None, ("row", "col")), P(), P(), P(), P(), P())
    return jax.shard_map(
        on_device, mesh=mesh, in_specs=in_specs, out_specs=out_specs, check_vma=False
    )
```

time: 893 us -> 512 us (0.57)
  matrix products: 282 us -> 3.93 us
  local copies, waits for them, and re-layouts: 133 us -> 43.7 us
  Pallas kernels: 0 us -> 42.8 us
  waiting for transfers between devices: 315 us -> 276 us
  blocking collectives: 131 us -> 119 us
    dot_general x77 -> x5, matrix products: 282 us -> 3.93 us  [the longest x1 1.06 us: on_device(): jnp.dot(first_agg, hidden_weight, preferred_element_type=jnp.float32)]
    all_gather x2 -> x0, waiting for transfers between devices: 84.8 us -> none  [the longest x1 54 us: on_device(): hidden_column = lax.all_gather(hidden, 'row', axis=0, tiled=True)]
    gather x36 -> x0, local copies, waits for them, and re-layouts: 84.4 us -> none  [one_group(): pieces = tiled[from_tile]]
    psum x2 -> x1, blocking collectives: 131 us -> 66.5 us  [on_device(): lax.psum((hidden_weight_part, jnp.sum(pre_grad, axis=0), class_weight_par...]
    psum x1, waiting for transfers between devices: 76.8 us -> 134 us  [on_device(): lax.psum((hidden_weight_part, jnp.sum(pre_grad, axis=0), class_weight_par...]
    all_gather x0 -> x2, blocking collectives: none -> 52.4 us  [the longest x1 30.5 us: on_device(): parts = lax.all_gather(score_part, 'row', axis=0)]
    while x98 -> x0, local copies, waits for them, and re-layouts: 43.4 us -> none
    pallas_call x0 -> x4, Pallas kernels: none -> 42.8 us  [the longest x1 24.3 us: densify(): pl.pallas_call(lambda *refs: densify_kernel(n_rows, *refs), out_shape=plt...]
  transfers between devices with their start and end apart: 7 -> 5, of which waited for: 6 -> 5; matrix products, arithmetic and copies ran while one was open for 0% -> 1% of each run, Pallas kernels for 0% -> 5%
where the time goes in v1:
time: 512 us; the launch traced here: 511 us
  waiting for transfers between devices  276 us (54%)
  blocking collectives  119 us (23%)
  local copies, waits for them, and re-layouts  43.7 us (9%)
  Pallas kernels  42.8 us (8%)
  between operations  16.9 us (3%)
  other arithmetic  8.53 us (2%)
    psum x1, waiting for transfers between devices, on_device(): lax.psum((hidden_weight_part, jnp.sum(pre_grad, axis=0), class_weight_par...  134 us
    reduce_scatter x1, waiting for transfers between devices, on_device(): back = lax.psum_scatter(back_term, 'row', scatter_dimension=0)  73.5 us
    psum x1, blocking collectives, on_device(): lax.psum((hidden_weight_part, jnp.sum(pre_grad, axis=0), class_weight_par...  66.5 us
    unnamed x30, local copies, waits for them, and re-layouts  43.7 us
    reduce_scatter x1, waiting for transfers between devices, on_device(): lax.psum_scatter(first_term, 'col', scatter_dimension=0, tiled=True)  31 us
    all_gather x1, blocking collectives, on_device(): parts = lax.all_gather(score_part, 'row', axis=0)  30.5 us
    reduce_scatter x1, waiting for transfers between devices, on_device(): scores = lax.psum_scatter(second_term, 'col', scatter_dimension=0)  25.8 us
    pallas_call x1, Pallas kernels, densify(): pl.pallas_call(lambda *refs: densify_kernel(n_rows, *refs), out_shape=plt...  24.3 us
  transfers between devices with their start and end apart: 5, of which 5 were waited for; matrix products, arithmetic and copies ran while one was open for 1% of the time, Pallas kernels for 5%

profile of v1, /device:TPU:1, one launch (start us, length us, event | category | flops | bytes accessed | tf_op | source)
XLA Modules:
  0.0 510.8 jit_solution(8277195387403249814)
XLA Ops:
  10.0 4.6 copy-done.5
  14.6 24.3 %densify.1.refs_0_ = bf16[896,128,128]{2,1,0:T(8,128)(2,1)S(1)} custom-call(s32[384]{0:T(512)S(1)} %reduce.refs_0_, s32[384]{0:T(512)S(1)} %reduce.1.refs_1_, s32[1,1]{1,0:T(1,128)S(6)} %copy.19.refs_2_, bf16[384,128,128]{2,1,0:T(8,128)(2,1)S(1)} %bitcast.23), custom_call_target="tpu_custom_call" | custom-call | tf_op jit(solution)/shard_map/densify/pallas_call | solution.py:71
  39.0 9.8 %copy-done.1 = bf16[896,128,128]{2,1,0:T(8,128)(2,1)} copy-done((bf16[896,128,128]{2,1,0:T(8,128)(2,1)}, bf16[896,128,128]{2,1,0:T(8,128)(2,1)S(1)}, u32[]{:S(2)}) %copy-start.1) | copy-done | bytes 29360152
  48.8 10.5 %all-gather.4.cloned.1.call-done.refs_1_ = bf16[4096,128]{1,0:T(8,128)(2,1)} async-done(((bf16[256,128]{1,0:T(8,128)(2,1)}), bf16[4096,128]{1,0:T(8,128)(2,1)}) %all-gather.4.cloned.1.call-update) | async-done | bytes 1048592 | tf_op jit(solution)/shard_map/all_gather | solution.py:165
  59.3 9.3 %copy-done.2 = bf16[896,128,128]{2,1,0:T(8,128)(2,1)S(1)} copy-done((bf16[896,128,128]{2,1,0:T(8,128)(2,1)S(1)}, bf16[896,128,128]{2,1,0:T(8,128)(2,1)}, u32[]{:S(2)}) %copy-start.2) | copy-done | bytes 29360152
  68.7 1.2 copy-done.6
  69.9 6.4 %first.1 = bf16[2048,128]{1,0:T(8,128)(2,1)} custom-call(bf16[896,128,128]{2,1,0:T(8,128)(2,1)S(1)} %copy-done.2, bf16[4096,128]{1,0:T(8,128)(2,1)S(1)} %copy-done.6), custom_call_target="tpu_custom_call" | custom-call | tf_op jit(solution)/shard_map/first/pallas_call | solution.py:137
  76.4 31.0 %reduce-scatter.4.cloned.1.call-done = bf16[256,128]{1,0:T(8,128)(2,1)} async-done(((bf16[2048,128]{1,0:T(8,128)(2,1)}), bf16[256,128]{1,0:T(8,128)(2,1)}) %reduce-scatter.4.cloned.1.call-update) | async-done | bytes 65552 | tf_op jit(solution)/shard_map/reduce_scatter | solution.py:169
  107.4 1.1 multiply_convert_fusion
  108.6 30.5 %all-gather = bf16[768,256]{1,0:T(8,128)(2,1)S(1)} all-gather(bf16[48,256]{1,0:T(8,128)(2,1)S(1)} %convolution_convert_fusion), channel_id=2, replica_groups=mesh['row'=16,'col'=8] {'row'}, dimensions={0}, use_global_device_ids=true | all-gather | bytes 417792 | tf_op jit(solution)/shard_map/all_gather | solution.py:178
  139.2 9.3 %copy-done.3 = bf16[896,128,128]{2,1,0:T(8,128)(2,1)S(1)} copy-done((bf16[896,128,128]{2,1,0:T(8,128)(2,1)S(1)}, bf16[896,128,128]{2,1,0:T(8,128)(2,1)}, u32[]{:S(2)}) %copy-start.3) | copy-done | bytes 29360152
  148.5 6.5 %second.1 = bf16[8,48,256]{2,1,0:T(8,128)(2,1)} custom-call(bf16[896,128,128]{2,1,0:T(8,128)(2,1)S(1)} %copy-done.3, bf16[16,48,256]{2,1,0:T(8,128)(2,1)S(1)} %bitcast.24), custom_call_target="tpu_custom_call" | custom-call | tf_op jit(solution)/shard_map/second/pallas_call | solution.py:137
  155.1 25.8 %reduce-scatter.6.cloned.1.call-done = bf16[1,48,256]{2,1,0:T(8,128)(2,1)} async-done(((bf16[8,48,256]{2,1,0:T(8,128)(2,1)}), bf16[1,48,256]{2,1,0:T(8,128)(2,1)}) %reduce-scatter.6.cloned.1.call-update) | async-done | bytes 24592 | tf_op jit(solution)/shard_map/reduce_scatter | solution.py:180
  182.0 21.9 %all-gather.1 = bf16[384,256]{1,0:T(8,128)(2,1)S(1)} all-gather(bf16[48,256]{1,0:T(8,128)(2,1)S(1)} %pad.10), channel_id=3, replica_groups=mesh['row'=16,'col'=8] {'col'}, dimensions={0}, use_global_device_ids=true | all-gather | bytes 221184 | tf_op jit(solution)/shard_map/all_gather | solution.py:189
  203.9 9.3 %copy-done.4 = bf16[896,128,128]{2,1,0:T(8,128)(2,1)S(1)} copy-done((bf16[896,128,128]{2,1,0:T(8,128)(2,1)S(1)}, bf16[896,128,128]{2,1,0:T(8,128)(2,1)}, u32[]{:S(2)}) %copy-start.4) | copy-done | bytes 29360152
  213.3 5.5 %back.1 = bf16[16,48,256]{2,1,0:T(8,128)(2,1)} custom-call(bf16[896,128,128]{2,1,0:T(8,128)(2,1)S(1)} %copy-done.4, bf16[8,48,256]{2,1,0:T(8,128)(2,1)S(1)} %bitcast.25), custom_call_target="tpu_custom_call" | custom-call | tf_op jit(solution)/shard_map/back/pallas_call | solution.py:137
  219.4 73.5 %reduce-scatter.8.cloned.1.call-done = bf16[1,48,256]{2,1,0:T(8,128)(2,1)} async-done(((bf16[16,48,256]{2,1,0:T(8,128)(2,1)}), bf16[1,48,256]{2,1,0:T(8,128)(2,1)}) %reduce-scatter.8.cloned.1.call-update) | async-done | bytes 24592 | tf_op jit(solution)/shard_map/reduce_scatter | solution.py:191
  293.8 1.0 fusion.12
  294.8 66.5 %all-reduce.2 = (f32[]{:T(128)}, f32[]{:T(128)}, f32[256]{0:T(256)S(1)}, f32[256,47]{0,1:T(8,128)S(1)}, f32[47]{0:T(128)S(1)}) all-reduce(f32[]{:T(128)} %get-tuple-element.10, f32[]{:T(128)} %get-tuple-element.9, f32[256]{0:T(256)S(1)} %get-tuple-element.21, ...), channel_id=1, replica_groups=mesh['row'=16,'col'=8] {'row','col'}, use_global_device_ids=true, to_apply=%region_6.7 | all-reduce | flops 12337 | bytes 98696 | tf_op jit(solution)/shard_map/psum | solution.py:203
  361.3 1.2 broadcast_divide_fusion.1
  362.4 1.1 broadcast_divide_fusion.2
  364.5 1.1 broadcast_divide_fusion.3
  366.8 134.3 %all-reduce.5.cloned.1.call-done = f32[128,256]{1,0:T(8,128)} async-done(((f32[128,256]{1,0:T(8,128)}), f32[128,256]{1,0:T(8,128)}) %all-reduce.5.cloned.1.call-update) | async-done | bytes 131088 | tf_op jit(solution)/shard_map/psum | solution.py:203
  501.0 2.1 broadcast_divide_fusion
  (46 shorter events, 5.9 us)
Async XLA Ops:
  7.2 100.2 %copy-start = (bf16[128,256]{1,0:T(8,128)(2,1)S(1)}, bf16[128,256]{1,0:T(8,128)(2,1)}, u32[]{:S(2)}) copy-start(bf16[128,256]{1,0:T(8,128)(2,1)} %param.18) | copy-start | bytes 196612
  7.2 52.1 %all-gather.4.cloned.1.call-start = ((), (), s32[]{:S(2)}) async-start(), calls=%async_computation.3 | async-start | bytes 1114112 | tf_op jit(solution)/shard_map/all_gather | solution.py:165
  7.9 99.5 %reduce-scatter.4.cloned.1.call-start = ((), (), s32[]{:S(2)}) async-start(), calls=%async_computation.4 | async-start | bytes 589824 | tf_op jit(solution)/shard_map/reduce_scatter | solution.py:169
  10.0 4.6 copy-start.5
  14.6 92.8 %copy-start.14 = (f32[256]{0:T(256)S(1)}, f32[256]{0:T(256)}, u32[]{:S(2)}) copy-start(f32[256]{0:T(256)} %param.19) | copy-start | bytes 3076
  14.6 93.9 %copy-start.10 = (bf16[256,47]{0,1:T(8,128)(2,1)S(1)}, bf16[256,47]{0,1:T(8,128)(2,1)}, u32[]{:S(2)}) copy-start(bf16[256,47]{0,1:T(8,128)(2,1)} %param.20) | copy-start | bytes 72196
  38.9 9.8 %copy-start.1 = (bf16[896,128,128]{2,1,0:T(8,128)(2,1)}, bf16[896,128,128]{2,1,0:T(8,128)(2,1)S(1)}, u32[]{:S(2)}) copy-start(bf16[896,128,128]{2,1,0:T(8,128)(2,1)S(1)} %densify.1.refs_0_) | copy-start | bytes 88080384
  59.3 9.4 %copy-start.2 = (bf16[896,128,128]{2,1,0:T(8,128)(2,1)S(1)}, bf16[896,128,128]{2,1,0:T(8,128)(2,1)}, u32[]{:S(2)}) copy-start(bf16[896,128,128]{2,1,0:T(8,128)(2,1)} %copy-done.1) | copy-start | bytes 88080384
  68.6 1.2 copy-start.6
  69.9 85.2 %copy-start.11 = (s32[256]{0:T(256)S(1)}, s32[256]{0:T(256)}, u32[]{:S(2)}) copy-start(s32[256]{0:T(256)} %param.17) | copy-start | bytes 3076
  69.9 111.1 %copy-start.13 = (f32[47]{0:T(128)S(1)}, f32[47]{0:T(128)}, u32[]{:S(2)}) copy-start(f32[47]{0:T(128)} %param.21) | copy-start | bytes 568
  69.9 112.0 %copy-start.12 = (s32[256]{0:T(256)S(1)}, s32[256]{0:T(256)}, u32[]{:S(2)}) copy-start(s32[256]{0:T(256)} %param.16) | copy-start | bytes 3076
  76.3 104.6 %reduce-scatter.6.cloned.1.call-start = ((), (), s32[]{:S(2)}) async-start(), calls=%async_computation.5 | async-start | bytes 221184 | tf_op jit(solution)/shard_map/reduce_scatter | solution.py:180
  108.4 184.5 %copy-start.7 = (bf16[256,256]{1,0:T(8,128)(2,1)}, bf16[256,256]{1,0:T(8,128)(2,1)S(1)}, u32[]{:S(2)}) copy-start(bf16[256,256]{1,0:T(8,128)(2,1)S(1)} %get-tuple-element.19) | copy-start | bytes 393220
  139.1 9.4 %copy-start.3 = (bf16[896,128,128]{2,1,0:T(8,128)(2,1)S(1)}, bf16[896,128,128]{2,1,0:T(8,128)(2,1)}, u32[]{:S(2)}) copy-start(bf16[896,128,128]{2,1,0:T(8,128)(2,1)} %copy-done.1) | copy-start | bytes 88080384
  148.5 215.1 %copy-start.9 = (bf16[256,128]{1,0:T(8,128)(2,1)S(1)}, bf16[256,128]{1,0:T(8,128)(2,1)}, u32[]{:S(2)}) copy-start(bf16[256,128]{1,0:T(8,128)(2,1)} %reduce-scatter.4.cloned.1.call-done) | copy-start | bytes 196612
  155.1 137.9 %reduce-scatter.8.cloned.1.call-start = ((), (), s32[]{:S(2)}) async-start(), calls=%async_computation.6 | async-start | bytes 417792 | tf_op jit(solution)/shard_map/reduce_scatter | solution.py:191
  181.8 321.4 %copy-start.8 = (f32[47,256]{1,0:T(8,128)}, f32[47,256]{1,0:T(8,128)S(1)}, u32[]{:S(2)}) copy-start(f32[47,256]{1,0:T(8,128)S(1)} %get-tuple-element.17) | copy-start | bytes 144388
  203.9 9.4 %copy-start.4 = (bf16[896,128,128]{2,1,0:T(8,128)(2,1)S(1)}, bf16[896,128,128]{2,1,0:T(8,128)(2,1)}, u32[]{:S(2)}) copy-start(bf16[896,128,128]{2,1,0:T(8,128)(2,1)} %copy-done.1) | copy-start | bytes 88080384
  218.8 282.3 %all-reduce.5.cloned.1.call-start = ((), (), s32[]{:S(2)}) async-start(), calls=%async_computation.7 | async-start | bytes 262144 | tf_op jit(solution)/shard_map/psum | solution.py:203
Sparse Core Ops, SparseCore 0:
  10.5 48.7 all-gather.3
  76.4 30.8 reduce-scatter.3
  155.2 25.7 reduce-scatter.5
  218.9 73.9 reduce-scatter.7
  364.6 136.4 all-reduce.4

commit v2 on v1

v2 whole, which is shorter than its diff:
```python
import jax
import jax.numpy as jnp
from jax import lax
from jax.experimental import pallas as pl
from jax.experimental.pallas import tpu as pltpu
from jax.sharding import PartitionSpec as P

TILE = 128
PADDED = 48
MESH = pl.DeviceIdType.MESH
NT = (((1,), (1,)), ((), ()))
TN = (((0,), (0,)), ((), ()))


def densify_kernel(n_rows, rows, cols, count, values, out, head, nxt, dups, sem):
    slots = values.shape[0]
    places = out.shape[0] - slots
    live = count[0, 0]
    zero = jnp.zeros((TILE, TILE), jnp.bfloat16)

    def clear(p, _):
        head[p] = -1
        out[p] = zero
        return 0

    lax.fori_loop(0, places, clear, 0, unroll=8)

    def place(s, found):
        p = cols[0, 0, s] * n_rows + rows[0, 0, s]
        alive = s < live
        before = head[p]
        first = jnp.logical_and(alive, before < 0)
        again = jnp.logical_and(alive, before >= 0)
        head[p] = jnp.where(alive, s, before)
        nxt[s] = before
        dups[found] = p
        pltpu.make_async_copy(
            values.at[s], out.at[jnp.where(first, p, places + s)], sem
        ).start()
        return found + again.astype(jnp.int32)

    found = lax.fori_loop(0, slots, place, 0, unroll=8)
    pltpu.make_async_copy(values, out.at[pl.ds(places, slots)], sem).wait()

    def merge(i, _):
        p = dups[i]
        top = head[p]

        @pl.when(top >= 0)
        def _():
            head[p] = -1

            def more(state):
                return nxt[state[0]] >= 0

            def add(state):
                s, total = state
                return nxt[s], total + out[places + s].astype(jnp.float32)

            _, total = lax.while_loop(more, add, (top, out[p].astype(jnp.float32)))
            out[p] = total.astype(jnp.bfloat16)

        return 0

    lax.fori_loop(0, found, merge, 0)


def densify(rows, cols, count, values, n_rows, n_cols):
    slots = values.shape[0]
    places = n_rows * n_cols
    smem = pl.BlockSpec(memory_space=pltpu.SMEM)
    return pl.pallas_call(
        lambda *refs: densify_kernel(n_rows, *refs),
        out_shape=pltpu.VMEM((places + slots, TILE, TILE), jnp.bfloat16),
        in_specs=[smem, smem, smem, pl.BlockSpec(memory_space=pltpu.HBM)],
        out_specs=pl.BlockSpec(memory_space=pltpu.VMEM),
        scratch_shapes=[
            pltpu.SMEM((places,), jnp.int32),
            pltpu.SMEM((slots,), jnp.int32),
            pltpu.SMEM((slots + 1,), jnp.int32),
            pltpu.SemaphoreType.DMA,
        ],
        compiler_params=pltpu.CompilerParams(vmem_limit_bytes=4 * 2**20),
        name="densify",
    )(rows, cols, count, pltpu.with_memory_space_constraint(values, pltpu.HBM))


class Exchange:
    def __init__(self, axis, size, dst, send_sem, recv_sem):
        self.axis, self.size, self.dst = axis, size, dst
        self.send_sem, self.recv_sem = send_sem, recv_sem
        self.me = lax.axis_index(axis)

    def copy(self, source, slot, peer):
        return pltpu.make_async_remote_copy(
            src_ref=source,
            dst_ref=self.dst.at[slot],
            send_sem=self.send_sem.at[peer],
            recv_sem=self.recv_sem.at[slot],
            device_id={self.axis: peer},
            device_id_type=MESH,
        )

    def peers(self, body):
        def step(d, _):
            body(lax.rem(self.me + d, self.size))
            return 0

        lax.fori_loop(1, self.size, step, 0)

    def send(self, source, peer):
        self.copy(source, self.me, peer).start()

    def send_all(self, source_of):
        self.peers(lambda peer: self.send(source_of(peer), peer))

    def receive_all(self):
        self.peers(lambda peer: self.copy(self.dst.at[peer], peer, peer).wait_recv())

    def sent_all(self):
        self.peers(lambda peer: self.copy(self.dst.at[peer], self.me, peer).wait_send())


def rows_of(dense, i, n_rows, n_cols):
    return jnp.concatenate(
        [dense[pl.ds(k * n_rows + 2 * i, 2)].reshape(2 * TILE, TILE) for k in range(n_cols)],
        axis=1,
    )


def cols_of(dense, k, n_rows):
    return jnp.concatenate(
        [
            dense[pl.ds((2 * k + h) * n_rows, n_rows)].reshape(n_rows * TILE, TILE)
            for h in range(2)
        ],
        axis=1,
    )


def step_kernel(
    R,
    C,
    x,
    dense,
    labels,
    mask,
    w1,
    b1,
    w2,
    b2,
    hidden_out,
    logits_out,
    loss_out,
    w1_grad_out,
    b1_grad_out,
    w2_grad_out,
    b2_grad_out,
    xg,
    t1,
    r1,
    s2,
    hw,
    t2,
    r2,
    s3,
    gg,
    t3,
    r3,
    part,
    r4,
    s5,
    r5,
    fin,
    pre,
    agg,
    w2s,
    b2s,
    send_sems,
    recv_sems,
):
    n_rows, n_cols = 2 * C, 2 * R
    nodes = x.shape[0]
    classes = w2.shape[0]
    piece = fin.shape[1]
    row, col = lax.axis_index("row"), lax.axis_index("col")

    barrier = pltpu.get_barrier_semaphore()

    def greet(axis, me, size):
        def one(d, _):
            pl.semaphore_signal(
                barrier,
                inc=1,
                device_id={axis: lax.rem(me + d, size)},
                device_id_type=MESH,
            )
            return 0

        lax.fori_loop(1, size, one, 0)

    greet("row", row, R)
    greet("col", col, C)

    def exchange(number, axis, size, dst):
        return Exchange(axis, size, dst, send_sems.at[number], recv_sems.at[number])

    ex_x = exchange(0, "row", R, xg)
    ex_first = exchange(1, "col", C, r1)
    ex_hw = exchange(2, "row", R, hw)
    ex_second = exchange(3, "col", C, r2)
    ex_grad = exchange(4, "col", C, gg)
    ex_back = exchange(5, "row", R, r3)
    ex_part = exchange(6, "row", R, r4)
    ex_sum = exchange(7, "col", C, r5)
    ex_fin = exchange(8, "row", R, fin)

    xg[row] = x[...]
    w2s[...] = jnp.zeros_like(w2s)
    w2s[0:classes, :] = w2[...].astype(jnp.float32)
    b2s[...] = jnp.zeros_like(b2s)
    b2s[0:1, 0:classes] = b2[...]
    pl.semaphore_wait(barrier, R + C - 2)

    ex_x.send_all(lambda peer: x)
    ex_x.receive_all()

    source = xg.reshape(R * nodes, x.shape[1])

    def first(d, _):
        peer = lax.rem(col + d, C)
        t1[peer] = jnp.dot(
            rows_of(dense, peer, n_rows, n_cols), source[...], preferred_element_type=jnp.float32
        ).astype(t1.dtype)

        @pl.when(d < C)
        def _():
            ex_first.send(t1.at[peer], peer)

        return 0

    lax.fori_loop(1, C + 1, first, 0)
    r1[col] = t1[col]
    ex_first.receive_all()

    def add_up(ref, size):
        return lax.fori_loop(
            1,
            size,
            lambda j, total: total + ref[j].astype(jnp.float32),
            ref[0].astype(jnp.float32),
        )

    agg[...] = add_up(r1, C).astype(jnp.bfloat16)
    v = jnp.dot(agg[...], w1[...], preferred_element_type=jnp.float32) + b1[...]
    pre[...] = v
    hidden_out[...] = (v / (1.0 + jnp.exp(-v))).astype(jnp.bfloat16)
    s2[...] = lax.dot_general(
        w2s[...].astype(jnp.bfloat16), hidden_out[...], NT, preferred_element_type=jnp.float32
    ).astype(jnp.bfloat16)

    hw[row] = s2[...]
    ex_hw.send_all(lambda peer: s2)
    ex_hw.receive_all()

    def second(d, _):
        peer = lax.rem(col + d, C)
        left = jnp.concatenate([hw[k] for k in range(R)], axis=1)
        t2[peer] = lax.dot_general(
            left, rows_of(dense, peer, n_rows, n_cols), NT, preferred_element_type=jnp.float32
        ).astype(t2.dtype)

        @pl.when(d < C)
        def _():
            ex_second.send(t2.at[peer], peer)

        return 0

    lax.fori_loop(1, C + 1, second, 0)
    r2[col] = t2[col]
    ex_second.receive_all()

    turned = jnp.transpose(jnp.broadcast_to(b2s[0:1, :], (TILE, TILE)))[0:PADDED, :]
    logits = add_up(r2, C) + jnp.concatenate([turned] * (nodes // TILE), axis=1)
    logits_out[...] = logits[0:classes, :]
    index = lax.broadcasted_iota(jnp.int32, (PADDED, nodes), 0)
    real = index < classes
    top = jnp.max(jnp.where(real, logits, -jnp.inf), axis=0, keepdims=True)
    terms = jnp.where(real, jnp.exp(logits - top), 0.0)
    log_total = top + jnp.log(jnp.sum(terms, axis=0, keepdims=True))
    onehot = (index == labels[...]).astype(jnp.float32)
    weights = mask[...].astype(jnp.float32)
    cross = weights * (log_total - jnp.sum(onehot * logits, axis=0, keepdims=True))
    grad = jnp.where(real, jnp.exp(logits - log_total) - onehot, 0.0) * weights
    s3[...] = grad.astype(jnp.bfloat16)

    gg[col] = s3[...]
    ex_grad.send_all(lambda peer: s3)

    def halves(base, value):
        height = value.shape[0]
        for h in range(2):
            part[pl.ds(base + h * height, height), :] = value[:, h * TILE : (h + 1) * TILE]

    base2, base3 = 2 * w1.shape[0], 2 * w1.shape[0] + 2 * PADDED
    ones = jnp.ones((8, nodes), jnp.float32)
    b2_part = lax.dot_general(
        ones, grad, NT, precision=lax.Precision.HIGHEST, preferred_element_type=jnp.float32
    )
    part[pl.ds(base3, 32), :] = jnp.zeros((32, TILE), jnp.float32)
    part[pl.ds(base3 + 8, 1), 0:PADDED] = b2_part[0:1, :]
    part[pl.ds(base3 + 16, 1), :] = jnp.broadcast_to(
        jnp.sum(cross, axis=1, keepdims=True), (1, TILE)
    )
    part[pl.ds(base3 + 24, 1), :] = jnp.broadcast_to(
        jnp.sum(weights, axis=1, keepdims=True), (1, TILE)
    )
    ex_grad.receive_all()

    def back(d, _):
        peer = lax.rem(row + d, R)
        left = jnp.concatenate([gg[k] for k in range(C)], axis=1)
        t3[peer] = jnp.dot(
            left, cols_of(dense, peer, n_rows), preferred_element_type=jnp.float32
        ).astype(t3.dtype)

        @pl.when(d < R)
        def _():
            ex_back.send(t3.at[peer], peer)

        return 0

    lax.fori_loop(1, R + 1, back, 0)
    r3[row] = t3[row]
    ex_back.receive_all()

    turned_grad = add_up(r3, R).astype(jnp.bfloat16)
    hidden_grad = lax.dot_general(
        turned_grad, w2s[...].astype(jnp.bfloat16), TN, preferred_element_type=jnp.float32
    )
    v = pre[...]
    s = 1.0 / (1.0 + jnp.exp(-v))
    pre_grad = hidden_grad * s * (1.0 + v * (1.0 - s))
    b1_part = jnp.sum(pre_grad, axis=0, keepdims=True)
    for h in range(2):
        part[pl.ds(base3 + h, 1), :] = b1_part[:, h * TILE : (h + 1) * TILE]
    halves(
        0,
        lax.dot_general(
            agg[...], pre_grad.astype(jnp.bfloat16), TN, preferred_element_type=jnp.float32
        ),
    )
    halves(
        base2,
        jnp.dot(turned_grad, hidden_out[...], preferred_element_type=jnp.float32),
    )

    ex_part.send_all(lambda peer: part.at[pl.ds(peer * piece, piece)])
    r4[row] = part[pl.ds(row * piece, piece), :]
    ex_part.receive_all()
    s5[...] = add_up(r4, R)
    r5[col] = s5[...]
    ex_sum.send_all(lambda peer: s5)
    ex_sum.receive_all()
    s5_total = add_up(r5, C)
    fin[row] = s5_total
    ex_fin.send_all(lambda peer: fin.at[row])
    ex_fin.receive_all()

    whole = fin.reshape(R * piece, TILE)
    count = whole[base3 + 24 : base3 + 25, 0:1]
    for h in range(2):
        lanes = slice(h * TILE, (h + 1) * TILE)
        height = w1.shape[0]
        w1_grad_out[:, lanes] = whole[h * height : (h + 1) * height, :] / count
        low = base2 + h * PADDED
        w2_grad_out[:, lanes] = whole[low : low + classes, :] / count
        b1_grad_out[:, lanes] = whole[base3 + h : base3 + h + 1, :] / count
    b2_grad_out[...] = whole[base3 + 8 : base3 + 9, 0:classes] / count
    loss_out[...] = whole[base3 + 16 : base3 + 17, 0:1] / count

    for ex in (ex_x, ex_first, ex_hw, ex_second, ex_grad, ex_back, ex_part, ex_sum, ex_fin):
        ex.sent_all()


def on_device(
    node_features,
    tile_values,
    tile_rows,
    tile_cols,
    tile_count,
    labels,
    train_mask,
    hidden_weight,
    hidden_bias,
    class_weight,
    class_bias,
):
    nodes, features = node_features.shape
    hidden, classes = class_weight.shape
    R, C = lax.axis_size("row"), lax.axis_size("col")
    n_rows, n_cols = C * nodes // TILE, R * nodes // TILE
    dense = densify(tile_rows, tile_cols, tile_count, tile_values[0, 0], n_rows, n_cols)
    used = 2 * features + 2 * PADDED + 32
    piece = -(-used // (8 * R)) * 8
    vmem = pl.BlockSpec(memory_space=pltpu.VMEM)
    bf16, f32 = jnp.bfloat16, jnp.float32
    out = lambda shape, kind: jax.ShapeDtypeStruct(shape, kind)
    scratch = [
        pltpu.VMEM((R, nodes, features), bf16),
        pltpu.VMEM((C, nodes, features), bf16),
        pltpu.VMEM((C, nodes, features), bf16),
        pltpu.VMEM((PADDED, nodes), bf16),
        pltpu.VMEM((R, PADDED, nodes), bf16),
        pltpu.VMEM((C, PADDED, nodes), bf16),
        pltpu.VMEM((C, PADDED, nodes), bf16),
        pltpu.VMEM((PADDED, nodes), bf16),
        pltpu.VMEM((C, PADDED, nodes), bf16),
        pltpu.VMEM((R, PADDED, nodes), bf16),
        pltpu.VMEM((R, PADDED, nodes), bf16),
        pltpu.VMEM((R * piece, TILE), f32),
        pltpu.VMEM((R, piece, TILE), f32),
        pltpu.VMEM((piece, TILE), f32),
        pltpu.VMEM((C, piece, TILE), f32),
        pltpu.VMEM((R, piece, TILE), f32),
        pltpu.VMEM((nodes, hidden), f32),
        pltpu.VMEM((nodes, features), bf16),
        pltpu.VMEM((PADDED, hidden), f32),
        pltpu.VMEM((8, TILE), f32),
        pltpu.SemaphoreType.DMA((9, R)),
        pltpu.SemaphoreType.DMA((9, R)),
    ]
    hidden_out, logits, loss, w1_grad, b1_grad, w2_grad, b2_grad = pl.pallas_call(
        lambda *refs: step_kernel(R, C, *refs),
        out_shape=(
            out((nodes, hidden), bf16),
            out((classes, nodes), f32),
            out((1, 1), f32),
            out((features, hidden), f32),
            out((1, hidden), f32),
            out((classes, hidden), f32),
            out((1, classes), f32),
        ),
        in_specs=[vmem] * 8,
        out_specs=(vmem,) * 7,
        scratch_shapes=scratch,
        compiler_params=pltpu.CompilerParams(
            collective_id=0, has_side_effects=True, vmem_limit_bytes=24 * 2**20
        ),
        name="step",
    )(
        node_features,
        pltpu.with_memory_space_constraint(dense, pltpu.VMEM),
        labels.reshape(1, nodes),
        train_mask.reshape(1, nodes),
        hidden_weight,
        hidden_bias.reshape(1, hidden),
        class_weight.T,
        class_bias.reshape(1, classes),
    )
    return (
        hidden_out,
        logits,
        loss[0, 0],
        w1_grad,
        b1_grad[0],
        w2_grad.T,
        b2_grad[0],
    )


def solution(mesh):
    in_specs = (
        P(("row", "col"), None),
        P("row", "col", None, None, None),
        P("row", "col", None),
        P("row", "col", None),
        P("row", "col"),
        P(("row", "col")),
        P(("row", "col")),
        P(),
        P(),
        P(),
        P(),
    )
    out_specs = (P(("row", "col"), None), P(None, ("row", "col")), P(), P(), P(), P(), P())
    return jax.shard_map(
        on_device, mesh=mesh, in_specs=in_specs, out_specs=out_specs, check_vma=False
    )
```

time: 512 us -> 100 us (0.20)
  waiting for transfers between devices: 276 us -> 0 us
  blocking collectives: 119 us -> 0 us
  Pallas kernels: 42.8 us -> 91.7 us
  local copies, waits for them, and re-layouts: 43.7 us -> 5.01 us
  between operations: 16.9 us -> 3.19 us
  other arithmetic: 8.53 us -> 0 us
    psum x1 -> x0, waiting for transfers between devices: 134 us -> none  [on_device(): lax.psum((hidden_weight_part, jnp.sum(pre_grad, axis=0), class_weight_par...]
    reduce_scatter x3 -> x0, waiting for transfers between devices: 130 us -> none  [the longest x1 73.5 us: on_device(): back = lax.psum_scatter(back_term, 'row', scatter_dimension=0)]
    psum x1 -> x0, blocking collectives: 66.5 us -> none  [on_device(): lax.psum((hidden_weight_part, jnp.sum(pre_grad, axis=0), class_weight_par...]
    pallas_call x3 -> x1, Pallas kernels: 18.5 us -> 83.8 us  [on_device(): pl.pallas_call(lambda *refs: step_kernel(R, C, *refs), out_shape=(out((no...]
    all_gather x2 -> x0, blocking collectives: 52.4 us -> none  [the longest x1 30.5 us: on_device(): parts = lax.all_gather(score_part, 'row', axis=0)]
    unnamed x30 -> x24, local copies, waits for them, and re-layouts: 43.7 us -> 5.01 us
    pallas_call x1, Pallas kernels: 24.3 us -> 7.87 us  [densify(): pl.pallas_call(lambda *refs: densify_kernel(n_rows, *refs), out_shape=plt...]
    all_gather x1 -> x0, waiting for transfers between devices: 10.5 us -> none  [on_device(): gathered = lax.all_gather(node_features, 'row', axis=0, tiled=True)]
  transfers between devices with their start and end apart: 5 -> 0, of which waited for: 5 -> 0; matrix products, arithmetic and copies ran while one was open for 1% -> 0% of each run, Pallas kernels for 5% -> 0%
where the time goes in v2:
time: 100 us; the launch traced here: 99.9 us
  Pallas kernels  91.7 us (92%)
  local copies, waits for them, and re-layouts  5.01 us (5%)
  between operations  3.19 us (3%)
    pallas_call x1, Pallas kernels, on_device(): pl.pallas_call(lambda *refs: step_kernel(R, C, *refs), out_shape=(out((no...  83.8 us
    pallas_call x1, Pallas kernels, densify(): pl.pallas_call(lambda *refs: densify_kernel(n_rows, *refs), out_shape=plt...  7.87 us
    unnamed x24, local copies, waits for them, and re-layouts  5.01 us

profile of v2, /device:TPU:1, one launch (start us, length us, event | category | flops | bytes accessed | tf_op | source)
XLA Modules:
  0.0 99.9 jit_solution(7014929673773517183)
XLA Ops:
  0.6 0.0 copy-start.2
  0.6 0.0 copy-start.1
  0.7 0.0 copy-start
  1.3 0.0 copy-start.3
  1.4 0.7 copy-done.3
  2.0 0.0 copy-start.4
  2.0 0.7 copy-done.4
  2.7 0.0 copy-start.5
  2.7 0.0 copy-start.6
  2.7 7.9 %densify.1.refs_1_ = bf16[896,128,128]{2,1,0:T(8,128)(2,1)S(1)} custom-call(s32[1,1,384]{2,1,0:T(1,128)S(1)} %copy-done.3, s32[1,1,384]{2,1,0:T(1,128)S(1)} %copy-done.4, s32[1,1]{1,0:T(1,128)S(6)} %copy.25.refs_2_, bf16[384,128,128]{2,1,0:T(8,128)(2,1)} %bitcast.18), custom_call_target="tpu_custom_call" | custom-call | tf_op jit(solution)/shard_map/densify/pallas_call | solution.py:72
  10.6 0.0 copy-done.2
  10.6 0.0 copy-done.1
  10.6 0.0 copy-done
  10.6 0.0 copy-done.5
  10.6 0.0 copy-done.6
  10.6 0.0 copy-done.7
  10.7 0.0 copy-done.8
  10.7 83.8 %step.1 = (bf16[256,256]{1,0:T(8,128)(2,1)S(1)}, f32[47,256]{1,0:T(8,128)S(1)}, f32[1,1]{1,0:T(1,128)}, f32[128,256]{1,0:T(8,128)S(1)}, f32[1,256]{1,0:T(1,128)S...) custom-call(bf16[256,128]{1,0:T(8,128)(2,1)S(1)} %copy-done, bf16[896,128,128]{2,1,0:T(8,128)(2,1)S(1)} %densify.1.refs_1_, ...), custom_call_target="tpu_custom_call" | custom-call | tf_op jit(solution)/shard_map/step/pallas_call | solution.py:433
  94.5 0.7 copy.26
  95.1 0.6 copy.27
  96.4 0.7 copy.29
  97.1 0.6 copy.30
  97.6 0.6 copy.31
  98.2 0.5 copy.32
  (2 shorter events, 0.0 us)
Async XLA Ops:
  0.6 10.0 %copy-start.2 = (bf16[256,47]{0,1:T(8,128)(2,1)S(1)}, bf16[256,47]{0,1:T(8,128)(2,1)}, u32[]{:S(2)}) copy-start(bf16[256,47]{0,1:T(8,128)(2,1)} %param.20) | copy-start | bytes 72196
  0.6 10.0 %copy-start.1 = (bf16[128,256]{1,0:T(8,128)(2,1)S(1)}, bf16[128,256]{1,0:T(8,128)(2,1)}, u32[]{:S(2)}) copy-start(bf16[128,256]{1,0:T(8,128)(2,1)} %refs_4_.1) | copy-start | bytes 196612
  0.7 10.0 %copy-start = (bf16[256,128]{1,0:T(8,128)(2,1)S(1)}, bf16[256,128]{1,0:T(8,128)(2,1)}, u32[]{:S(2)}) copy-start(bf16[256,128]{1,0:T(8,128)(2,1)} %refs_0_.3) | copy-start | bytes 196612
  1.3 0.7 copy-start.3
  2.0 0.7 copy-start.4
  2.7 7.9 %copy-start.5 = (s32[256]{0:T(256)S(1)}, s32[256]{0:T(256)}, u32[]{:S(2)}) copy-start(s32[256]{0:T(256)} %param.16) | copy-start | bytes 3076
  2.7 7.9 %copy-start.6 = (s32[256]{0:T(256)S(1)}, s32[256]{0:T(256)}, u32[]{:S(2)}) copy-start(s32[256]{0:T(256)} %param.17) | copy-start | bytes 3076
  2.7 7.9 %copy-start.7 = (f32[256]{0:T(256)S(1)}, f32[256]{0:T(256)}, u32[]{:S(2)}) copy-start(f32[256]{0:T(256)} %param.19) | copy-start | bytes 3076
  2.7 7.9 %copy-start.8 = (f32[47]{0:T(128)S(1)}, f32[47]{0:T(128)}, u32[]{:S(2)}) copy-start(f32[47]{0:T(128)} %param.21) | copy-start | bytes 568

commit v3 on v2

--- a/solution.py
+++ b/solution.py
@@ -12,11 +12,18 @@
 TN = (((0,), (0,)), ((), ()))
 
 
-def densify_kernel(n_rows, rows, cols, count, values, out, head, nxt, dups, sem):
+def densify_kernel(n_rows, rows_in, cols_in, count, values, out, rows, cols, head, nxt, dups, sem, sems):
     slots = values.shape[0]
     places = out.shape[0] - slots
-    live = count[0, 0]
     zero = jnp.zeros((TILE, TILE), jnp.bfloat16)
+    loads = [
+        pltpu.make_async_copy(source, target, sems.at[i])
+        for i, (source, target) in enumerate(
+            ((rows_in, rows), (cols_in, cols))
+        )
+    ]
+    for load in loads:
+        load.start()
 
     def clear(p, _):
         head[p] = -1
@@ -24,6 +31,9 @@
         return 0
 
     lax.fori_loop(0, places, clear, 0, unroll=8)
+    for load in loads:
+        load.wait()
+    live = count[0, 0]
 
     def place(s, found):
         p = cols[0, 0, s] * n_rows + rows[0, 0, s]
@@ -68,21 +78,29 @@
 def densify(rows, cols, count, values, n_rows, n_cols):
     slots = values.shape[0]
     places = n_rows * n_cols
-    smem = pl.BlockSpec(memory_space=pltpu.SMEM)
+    hbm = pl.BlockSpec(memory_space=pltpu.HBM)
     return pl.pallas_call(
         lambda *refs: densify_kernel(n_rows, *refs),
         out_shape=pltpu.VMEM((places + slots, TILE, TILE), jnp.bfloat16),
-        in_specs=[smem, smem, smem, pl.BlockSpec(memory_space=pltpu.HBM)],
+        in_specs=[hbm, hbm, pl.BlockSpec(memory_space=pltpu.SMEM), hbm],
         out_specs=pl.BlockSpec(memory_space=pltpu.VMEM),
         scratch_shapes=[
+            pltpu.SMEM(rows.shape, jnp.int32),
+            pltpu.SMEM(cols.shape, jnp.int32),
             pltpu.SMEM((places,), jnp.int32),
             pltpu.SMEM((slots,), jnp.int32),
             pltpu.SMEM((slots + 1,), jnp.int32),
             pltpu.SemaphoreType.DMA,
+            pltpu.SemaphoreType.DMA((2,)),
         ],
         compiler_params=pltpu.CompilerParams(vmem_limit_bytes=4 * 2**20),
         name="densify",
-    )(rows, cols, count, pltpu.with_memory_space_constraint(values, pltpu.HBM))
+    )(
+        pltpu.with_memory_space_constraint(rows, pltpu.HBM),
+        pltpu.with_memory_space_constraint(cols, pltpu.HBM),
+        count,
+        pltpu.with_memory_space_constraint(values, pltpu.HBM),
+    )
 
 
 class Exchange:
@@ -91,12 +109,12 @@
         self.send_sem, self.recv_sem = send_sem, recv_sem
         self.me = lax.axis_index(axis)
 
-    def copy(self, source, slot, peer):
+    def copy(self, source, target, peer):
         return pltpu.make_async_remote_copy(
             src_ref=source,
-            dst_ref=self.dst.at[slot],
-            send_sem=self.send_sem.at[peer],
-            recv_sem=self.recv_sem.at[slot],
+            dst_ref=target,
+            send_sem=self.send_sem,
+            recv_sem=self.recv_sem,
             device_id={self.axis: peer},
             device_id_type=MESH,
         )
@@ -109,16 +127,35 @@
         lax.fori_loop(1, self.size, step, 0)
 
     def send(self, source, peer):
-        self.copy(source, self.me, peer).start()
+        self.copy(source, self.dst.at[self.me], peer).start()
 
     def send_all(self, source_of):
         self.peers(lambda peer: self.send(source_of(peer), peer))
 
+    def everything(self):
+        span = self.dst.at[pl.ds(0, self.size - 1)]
+        return self.copy(span, span, lax.rem(self.me + 1, self.size))
+
     def receive_all(self):
-        self.peers(lambda peer: self.copy(self.dst.at[peer], peer, peer).wait_recv())
+        self.everything().wait_recv()
 
     def sent_all(self):
-        self.peers(lambda peer: self.copy(self.dst.at[peer], self.me, peer).wait_send())
+        self.everything().wait_send()
+
+
+class Gather(Exchange):
+    def copy(self, source, target, peer, slot=None):
+        return pltpu.make_async_remote_copy(
+            src_ref=source,
+            dst_ref=target,
+            send_sem=self.send_sem,
+            recv_sem=self.recv_sem.at[self.me if slot is None else slot],
+            device_id={self.axis: peer},
+            device_id_type=MESH,
+        )
+
+    def receive(self, slot):
+        self.copy(self.dst.at[slot], self.dst.at[slot], slot, slot).wait_recv()
 
 
 def rows_of(dense, i, n_rows, n_cols):
@@ -135,6 +172,12 @@
             for h in range(2)
         ],
         axis=1,
+    )
+
+
+def add_up(ref, size):
+    return lax.fori_loop(
+        1, size, lambda j, total: total + ref[j].astype(jnp.float32), ref[0].astype(jnp.float32)
     )
 
 
@@ -151,11 +194,7 @@
     b2,
     hidden_out,
     logits_out,
-    loss_out,
-    w1_grad_out,
-    b1_grad_out,
-    w2_grad_out,
-    b2_grad_out,
+    sums_out,
     xg,
     t1,
     r1,
@@ -168,15 +207,22 @@
     t3,
     r3,
     part,
+    part16,
     r4,
     s5,
     r5,
     fin,
+    first_acc,
+    second_acc,
+    back_acc,
     pre,
     agg,
     w2s,
     b2s,
     send_sems,
+    x_sems,
+    hw_sems,
+    grad_sems,
     recv_sems,
 ):
     n_rows, n_cols = 2 * C, 2 * R
@@ -202,36 +248,60 @@
     greet("row", row, R)
     greet("col", col, C)
 
-    def exchange(number, axis, size, dst):
-        return Exchange(axis, size, dst, send_sems.at[number], recv_sems.at[number])
-
-    ex_x = exchange(0, "row", R, xg)
-    ex_first = exchange(1, "col", C, r1)
-    ex_hw = exchange(2, "row", R, hw)
-    ex_second = exchange(3, "col", C, r2)
-    ex_grad = exchange(4, "col", C, gg)
-    ex_back = exchange(5, "row", R, r3)
-    ex_part = exchange(6, "row", R, r4)
-    ex_sum = exchange(7, "col", C, r5)
-    ex_fin = exchange(8, "row", R, fin)
+    ex_x = Gather("row", R, xg, send_sems.at[0], x_sems)
+    ex_first = Exchange("col", C, r1, send_sems.at[1], recv_sems.at[1])
+    ex_hw = Gather("row", R, hw, send_sems.at[2], hw_sems)
+    ex_second = Exchange("col", C, r2, send_sems.at[3], recv_sems.at[3])
+    ex_grad = Gather("col", C, gg, send_sems.at[4], grad_sems)
+    ex_back = Exchange("row", R, r3, send_sems.at[5], recv_sems.at[5])
+    ex_part = Exchange("col", C, r4, send_sems.at[6], recv_sems.at[6])
+    ex_sum = Exchange("row", R, r5, send_sems.at[7], recv_sems.at[7])
+    ex_fin = Exchange("col", C, fin, send_sems.at[8], recv_sems.at[8])
 
     xg[row] = x[...]
     w2s[...] = jnp.zeros_like(w2s)
     w2s[0:classes, :] = w2[...].astype(jnp.float32)
     b2s[...] = jnp.zeros_like(b2s)
     b2s[0:1, 0:classes] = b2[...]
+    first_acc[...] = jnp.zeros_like(first_acc)
+    second_acc[...] = jnp.zeros_like(second_acc)
+    back_acc[...] = jnp.zeros_like(back_acc)
     pl.semaphore_wait(barrier, R + C - 2)
 
-    ex_x.send_all(lambda peer: x)
-    ex_x.receive_all()
-
-    source = xg.reshape(R * nodes, x.shape[1])
+    core = lax.rem(row, 2)
+    beside = row + 1 - 2 * core
+
+    def send_x(d, _):
+        ex_x.send(x, lax.rem(row + 2 * d, R))
+        return 0
+
+    lax.fori_loop(1, R // 2, send_x, 0)
+    ex_x.send(x, beside)
+
+    def use_x(slot):
+        first_acc[...] += jnp.dot(
+            cols_of(dense, slot, n_rows), xg[slot], preferred_element_type=jnp.float32
+        )
+
+    use_x(row)
+    ex_x.receive(beside)
+    use_x(beside)
+
+    def pass_x(d, _):
+        slot = lax.rem(row + R - 2 * d, R)
+        ex_x.receive(slot)
+        ex_x.copy(xg.at[slot], xg.at[slot], beside, slot).start()
+        use_x(slot)
+        other = lax.rem(beside + R - 2 * d, R)
+        ex_x.receive(other)
+        use_x(other)
+        return 0
+
+    lax.fori_loop(1, R // 2, pass_x, 0)
 
     def first(d, _):
         peer = lax.rem(col + d, C)
-        t1[peer] = jnp.dot(
-            rows_of(dense, peer, n_rows, n_cols), source[...], preferred_element_type=jnp.float32
-        ).astype(t1.dtype)
+        t1[peer] = first_acc[pl.ds(peer * nodes, nodes), :].astype(t1.dtype)
 
         @pl.when(d < C)
         def _():
@@ -242,14 +312,6 @@
     lax.fori_loop(1, C + 1, first, 0)
     r1[col] = t1[col]
     ex_first.receive_all()
-
-    def add_up(ref, size):
-        return lax.fori_loop(
-            1,
-            size,
-            lambda j, total: total + ref[j].astype(jnp.float32),
-            ref[0].astype(jnp.float32),
-        )
 
     agg[...] = add_up(r1, C).astype(jnp.bfloat16)
     v = jnp.dot(agg[...], w1[...], preferred_element_type=jnp.float32) + b1[...]
@@ -261,14 +323,24 @@
 
     hw[row] = s2[...]
     ex_hw.send_all(lambda peer: s2)
-    ex_hw.receive_all()
+
+    def use_hw(d, _):
+        slot = lax.rem(row + R - d, R)
+
+        @pl.when(d > 0)
+        def _():
+            ex_hw.receive(slot)
+
+        second_acc[...] += lax.dot_general(
+            hw[slot], cols_of(dense, slot, n_rows), NT, preferred_element_type=jnp.float32
+        )
+        return 0
+
+    lax.fori_loop(0, R, use_hw, 0)
 
     def second(d, _):
         peer = lax.rem(col + d, C)
-        left = jnp.concatenate([hw[k] for k in range(R)], axis=1)
-        t2[peer] = lax.dot_general(
-            left, rows_of(dense, peer, n_rows, n_cols), NT, preferred_element_type=jnp.float32
-        ).astype(t2.dtype)
+        t2[peer] = second_acc[:, pl.ds(pl.multiple_of(peer * nodes, nodes), nodes)].astype(t2.dtype)
 
         @pl.when(d < C)
         def _():
@@ -308,21 +380,31 @@
         ones, grad, NT, precision=lax.Precision.HIGHEST, preferred_element_type=jnp.float32
     )
     part[pl.ds(base3, 32), :] = jnp.zeros((32, TILE), jnp.float32)
-    part[pl.ds(base3 + 8, 1), 0:PADDED] = b2_part[0:1, :]
-    part[pl.ds(base3 + 16, 1), :] = jnp.broadcast_to(
+    part[pl.ds(base3 + 2, 1), 0:PADDED] = b2_part[0:1, :]
+    part[pl.ds(base3 + 3, 1), :] = jnp.broadcast_to(
         jnp.sum(cross, axis=1, keepdims=True), (1, TILE)
     )
-    part[pl.ds(base3 + 24, 1), :] = jnp.broadcast_to(
+    part[pl.ds(base3 + 4, 1), :] = jnp.broadcast_to(
         jnp.sum(weights, axis=1, keepdims=True), (1, TILE)
     )
-    ex_grad.receive_all()
+
+    def use_grad(d, _):
+        slot = lax.rem(col + C - d, C)
+
+        @pl.when(d > 0)
+        def _():
+            ex_grad.receive(slot)
+
+        back_acc[...] += jnp.dot(
+            gg[slot], rows_of(dense, slot, n_rows, n_cols), preferred_element_type=jnp.float32
+        )
+        return 0
+
+    lax.fori_loop(0, C, use_grad, 0)
 
     def back(d, _):
         peer = lax.rem(row + d, R)
-        left = jnp.concatenate([gg[k] for k in range(C)], axis=1)
-        t3[peer] = jnp.dot(
-            left, cols_of(dense, peer, n_rows), preferred_element_type=jnp.float32
-        ).astype(t3.dtype)
+        t3[peer] = back_acc[:, pl.ds(pl.multiple_of(peer * nodes, nodes), nodes)].astype(t3.dtype)
 
         @pl.when(d < R)
         def _():
@@ -355,32 +437,78 @@
         jnp.dot(turned_grad, hidden_out[...], preferred_element_type=jnp.float32),
     )
 
-    ex_part.send_all(lambda peer: part.at[pl.ds(peer * piece, piece)])
-    r4[row] = part[pl.ds(row * piece, piece), :]
+    def split(value):
+        high = value.astype(jnp.bfloat16)
+        return high, (value - high.astype(jnp.float32)).astype(jnp.bfloat16)
+
+    last = C - 1
+    part16[pl.ds(0, base3), :] = part[pl.ds(0, base3), :].astype(jnp.bfloat16)
+    high, low = split(part[pl.ds(base3, 16), :])
+    part16[pl.ds(base3, 16), :] = high
+    part16[pl.ds(base3 + 16, 16), :] = low
+    ex_part.send_all(
+        lambda peer: part16.at[pl.ds(pl.multiple_of(peer * piece, piece), piece)]
+    )
+    r4[col] = part16[pl.ds(pl.multiple_of(col * piece, piece), piece), :]
     ex_part.receive_all()
-    s5[...] = add_up(r4, R)
-    r5[col] = s5[...]
+
+    def resplit(total):
+        high, low = split(total[piece - 32 : piece - 16, :] + total[piece - 16 :, :])
+        both = jnp.concatenate([high, low], axis=0)
+        plain = total.astype(jnp.bfloat16)
+        tail = jnp.where(col == last, both, plain[piece - 32 :, :])
+        return jnp.concatenate([plain[: piece - 32, :], tail], axis=0)
+
+    s5[...] = resplit(add_up(r4, C))
+    r5[row] = s5[...]
     ex_sum.send_all(lambda peer: s5)
     ex_sum.receive_all()
-    s5_total = add_up(r5, C)
-    fin[row] = s5_total
-    ex_fin.send_all(lambda peer: fin.at[row])
+
+    fin[col] = resplit(add_up(r5, R))
+    ex_fin.send_all(lambda peer: fin.at[col])
     ex_fin.receive_all()
 
-    whole = fin.reshape(R * piece, TILE)
-    count = whole[base3 + 24 : base3 + 25, 0:1]
+    for j in range(C):
+        sums_out[j * piece : (j + 1) * piece, :] = fin[j].astype(jnp.float32)
+    for ex in (ex_first, ex_hw, ex_second, ex_grad, ex_back, ex_part, ex_sum, ex_fin):
+        ex.sent_all()
+    ex_x.sent_all()
+
+
+def finish_kernel(
+    features,
+    classes,
+    hidden,
+    logits,
+    sums,
+    hidden_out,
+    logits_out,
+    loss_out,
+    w1_grad_out,
+    b1_grad_out,
+    w2_grad_out,
+    b2_grad_out,
+    sems,
+):
+    copies = [
+        pltpu.make_async_copy(hidden, hidden_out, sems.at[0]),
+        pltpu.make_async_copy(logits, logits_out, sems.at[1]),
+    ]
+    for copy in copies:
+        copy.start()
+    base2, base3 = 2 * features, 2 * features + 2 * PADDED
+    small = sums[base3 : base3 + 16, :] + sums[base3 + 16 : base3 + 32, :]
+    count = small[4:5, 0:1]
     for h in range(2):
         lanes = slice(h * TILE, (h + 1) * TILE)
-        height = w1.shape[0]
-        w1_grad_out[:, lanes] = whole[h * height : (h + 1) * height, :] / count
+        w1_grad_out[:, lanes] = sums[h * features : (h + 1) * features, :] / count
         low = base2 + h * PADDED
-        w2_grad_out[:, lanes] = whole[low : low + classes, :] / count
-        b1_grad_out[:, lanes] = whole[base3 + h : base3 + h + 1, :] / count
-    b2_grad_out[...] = whole[base3 + 8 : base3 + 9, 0:classes] / count
-    loss_out[...] = whole[base3 + 16 : base3 + 17, 0:1] / count
-
-    for ex in (ex_x, ex_first, ex_hw, ex_second, ex_grad, ex_back, ex_part, ex_sum, ex_fin):
-        ex.sent_all()
+        w2_grad_out[:, lanes] = sums[low : low + classes, :] / count
+        b1_grad_out[:, lanes] = small[h : h + 1, :] / count
+    b2_grad_out[...] = small[2:3, 0:classes] / count
+    loss_out[...] = small[3:4, 0:1] / count
+    for copy in copies:
+        copy.wait()
 
 
 def on_device(
@@ -402,8 +530,9 @@
     n_rows, n_cols = C * nodes // TILE, R * nodes // TILE
     dense = densify(tile_rows, tile_cols, tile_count, tile_values[0, 0], n_rows, n_cols)
     used = 2 * features + 2 * PADDED + 32
-    piece = -(-used // (8 * R)) * 8
+    piece = used // C
     vmem = pl.BlockSpec(memory_space=pltpu.VMEM)
+    hbm = pl.BlockSpec(memory_space=pltpu.HBM)
     bf16, f32 = jnp.bfloat16, jnp.float32
     out = lambda shape, kind: jax.ShapeDtypeStruct(shape, kind)
     scratch = [
@@ -418,31 +547,34 @@
         pltpu.VMEM((C, PADDED, nodes), bf16),
         pltpu.VMEM((R, PADDED, nodes), bf16),
         pltpu.VMEM((R, PADDED, nodes), bf16),
-        pltpu.VMEM((R * piece, TILE), f32),
-        pltpu.VMEM((R, piece, TILE), f32),
-        pltpu.VMEM((piece, TILE), f32),
-        pltpu.VMEM((C, piece, TILE), f32),
-        pltpu.VMEM((R, piece, TILE), f32),
+        pltpu.VMEM((used, TILE), f32),
+        pltpu.VMEM((used, TILE), bf16),
+        pltpu.VMEM((C, piece, TILE), bf16),
+        pltpu.VMEM((piece, TILE), bf16),
+        pltpu.VMEM((R, piece, TILE), bf16),
+        pltpu.VMEM((C, piece, TILE), bf16),
+        pltpu.VMEM((C * nodes, features), f32),
+        pltpu.VMEM((PADDED, C * nodes), f32),
+        pltpu.VMEM((PADDED, R * nodes), f32),
         pltpu.VMEM((nodes, hidden), f32),
         pltpu.VMEM((nodes, features), bf16),
         pltpu.VMEM((PADDED, hidden), f32),
         pltpu.VMEM((8, TILE), f32),
-        pltpu.SemaphoreType.DMA((9, R)),
-        pltpu.SemaphoreType.DMA((9, R)),
+        pltpu.SemaphoreType.DMA((9,)),
+        pltpu.SemaphoreType.DMA((R,)),
+        pltpu.SemaphoreType.DMA((R,)),
+        pltpu.SemaphoreType.DMA((C,)),
+        pltpu.SemaphoreType.DMA((9,)),
     ]
-    hidden_out, logits, loss, w1_grad, b1_grad, w2_grad, b2_grad = pl.pallas_call(
+    hidden_now, logits_now, sums = pl.pallas_call(
         lambda *refs: step_kernel(R, C, *refs),
         out_shape=(
-            out((nodes, hidden), bf16),
-            out((classes, nodes), f32),
-            out((1, 1), f32),
-            out((features, hidden), f32),
-            out((1, hidden), f32),
-            out((classes, hidden), f32),
-            out((1, classes), f32),
+            pltpu.VMEM((nodes, hidden), bf16),
+            pltpu.VMEM((classes, nodes), f32),
+            pltpu.VMEM((used, TILE), f32),
         ),
         in_specs=[vmem] * 8,
-        out_specs=(vmem,) * 7,
+        out_specs=(vmem,) * 3,
         scratch_shapes=scratch,
         compiler_params=pltpu.CompilerParams(
             collective_id=0, has_side_effects=True, vmem_limit_bytes=24 * 2**20
@@ -458,6 +590,23 @@
         class_weight.T,
         class_bias.reshape(1, classes),
     )
+    hidden_out, logits, loss, w1_grad, b1_grad, w2_grad, b2_grad = pl.pallas_call(
+        lambda *refs: finish_kernel(features, classes, *refs),
+        out_shape=(
+            out((nodes, hidden), bf16),
+            out((classes, nodes), f32),
+            out((1, 1), f32),
+            out((features, hidden), f32),
+            out((1, hidden), f32),
+            out((classes, hidden), f32),
+            out((1, classes), f32),
+        ),
+        in_specs=[vmem] * 3,
+        out_specs=(hbm, hbm) + (vmem,) * 5,
+        scratch_shapes=[pltpu.SemaphoreType.DMA((2,))],
+        compiler_params=pltpu.CompilerParams(vmem_limit_bytes=4 * 2**20),
+        name="finish",
+    )(*(pltpu.with_memory_space_constraint(a, pltpu.VMEM) for a in (hidden_now, logits_now, sums)))
     return (
         hidden_out,
         logits,

time: 100 us -> 91 us (0.910)
  local copies, waits for them, and re-layouts: 5.01 us -> 0.03 us
  Pallas kernels: 91.7 us -> 89.3 us
  between operations: 3.19 us -> 1.46 us
    unnamed x24 -> x14, local copies, waits for them, and re-layouts: 5.01 us -> 0.03 us
    pallas_call x1 -> x2, Pallas kernels: 83.8 us -> 82.1 us  [the longest x1 80.7 us: on_device(): pl.pallas_call(lambda *refs: step_kernel(R, C, *refs), out_shape=(pltpu.V...]
where the time goes in v3:
time: 91 us; the launch traced here: 90.8 us
  Pallas kernels  89.3 us (98%)
  between operations  1.46 us (2%)
    pallas_call x1, Pallas kernels, on_device(): pl.pallas_call(lambda *refs: step_kernel(R, C, *refs), out_shape=(pltpu.V...  80.7 us
    pallas_call x1, Pallas kernels, densify(): pl.pallas_call(lambda *refs: densify_kernel(n_rows, *refs), out_shape=plt...  7.26 us

profile of v3, /device:TPU:1, one launch (start us, length us, event | category | flops | bytes accessed | tf_op | source)
XLA Modules:
  0.0 90.8 jit_solution(17305229797321195440)
XLA Ops:
  0.6 0.0 copy-start.6
  0.6 0.0 copy-start.2
  0.7 0.0 copy-start.5
  0.7 0.0 copy-start.1
  0.7 0.0 copy-start.4
  0.7 0.0 copy-start.3
  0.7 0.0 copy-start
  1.4 7.3 %densify.1.refs_1_ = bf16[896,128,128]{2,1,0:T(8,128)(2,1)S(1)} custom-call(s32[1,1,384]{2,1,0:T(1,128)} %refs_0_.2, s32[1,1,384]{2,1,0:T(1,128)} %refs_1_.1, s32[1,1]{1,0:T(1,128)S(6)} %copy.18.refs_2_, bf16[384,128,128]{2,1,0:T(8,128)(2,1)} %bitcast.15), custom_call_target="tpu_custom_call" | custom-call | tf_op jit(solution)/shard_map/densify/pallas_call | solution.py:82
  8.7 0.0 copy-done.6
  8.7 0.0 copy-done.2
  8.7 0.0 copy-done.5
  8.7 0.0 copy-done.1
  8.7 0.0 copy-done.4
  8.7 0.0 copy-done.3
  8.7 0.0 copy-done
  8.7 80.7 %step.1 = (bf16[256,256]{1,0:T(8,128)(2,1)S(1)}, f32[47,256]{1,0:T(8,128)S(1)}, f32[384,128]{1,0:T(8,128)S(1)}) custom-call(bf16[256,128]{1,0:T(8,128)(2,1)S(1)} %copy-done, bf16[896,128,128]{2,1,0:T(8,128)(2,1)S(1)} %densify.1.refs_1_, s32[1,256]{1,0:T(1,128)S(1)} %bitcast.11, s32[1,256]{1,0:T(1,128)S(1)} %bitcast.12, bf16[128,256]{1,0:T(8,128)(2,1)S(1)} %copy-done.1, ...), custom_call_target="tpu_custom_call" | custom-call | tf_op jit(solution)/shard_map/step/pallas_call | solution.py:569
  89.5 1.3 %finish.1 = (bf16[256,256]{1,0:T(8,128)(2,1)}, f32[47,256]{1,0:T(8,128)}, f32[1,1]{1,0:T(1,128)}, f32[128,256]{1,0:T(8,128)}, f32[1,256]{1,0:T(1,128)}, /*index=5*/f32[47,256]{1,0:T(8,128)}, f32[1,47]{1,0:T(1,128)}) custom-call(bf16[256,256]{1,0:T(8,128)(2,1)S(1)} %get-tuple-element.17.refs_0_, f32[47,256]{1,0:T(8,128)S(1)} %get-tuple-element.18.refs_1_, ...), custom_call_target="tpu_custom_call" | custom-call | tf_op jit(solution)/shard_map/finish/pallas_call | solution.py:593
Async XLA Ops:
  0.6 8.0 %copy-start.6 = (f32[47]{0:T(128)S(1)}, f32[47]{0:T(128)}, u32[]{:S(2)}) copy-start(f32[47]{0:T(128)} %param.21) | copy-start | bytes 568
  0.6 8.0 %copy-start.2 = (bf16[256,47]{0,1:T(8,128)(2,1)S(1)}, bf16[256,47]{0,1:T(8,128)(2,1)}, u32[]{:S(2)}) copy-start(bf16[256,47]{0,1:T(8,128)(2,1)} %param.20) | copy-start | bytes 72196
  0.7 8.0 %copy-start.5 = (f32[256]{0:T(256)S(1)}, f32[256]{0:T(256)}, u32[]{:S(2)}) copy-start(f32[256]{0:T(256)} %param.19) | copy-start | bytes 3076
  0.7 8.0 %copy-start.1 = (bf16[128,256]{1,0:T(8,128)(2,1)S(1)}, bf16[128,256]{1,0:T(8,128)(2,1)}, u32[]{:S(2)}) copy-start(bf16[128,256]{1,0:T(8,128)(2,1)} %refs_4_.1) | copy-start | bytes 196612
  0.7 8.0 %copy-start.4 = (s32[256]{0:T(256)S(1)}, s32[256]{0:T(256)}, u32[]{:S(2)}) copy-start(s32[256]{0:T(256)} %param.17) | copy-start | bytes 3076
  0.7 8.0 %copy-start.3 = (s32[256]{0:T(256)S(1)}, s32[256]{0:T(256)}, u32[]{:S(2)}) copy-start(s32[256]{0:T(256)} %param.16) | copy-start | bytes 3076
  0.7 8.0 %copy-start = (bf16[256,128]{1,0:T(8,128)(2,1)S(1)}, bf16[256,128]{1,0:T(8,128)(2,1)}, u32[]{:S(2)}) copy-start(bf16[256,128]{1,0:T(8,128)(2,1)} %refs_0_.3) | copy-start | bytes 196612

commit v4 on v3

--- a/solution.py
+++ b/solution.py
@@ -12,9 +12,10 @@
 TN = (((0,), (0,)), ((), ()))
 
 
-def densify_kernel(n_rows, rows_in, cols_in, count, values, out, rows, cols, head, nxt, dups, sem, sems):
+def densify_kernel(n_rows, rows_in, cols_in, count, values, out, rows, cols, head, nxt, pairs, longer, sem, sems):
     slots = values.shape[0]
-    places = out.shape[0] - slots
+    places = head.shape[0]
+    spare = places + slots
     zero = jnp.zeros((TILE, TILE), jnp.bfloat16)
     loads = [
         pltpu.make_async_copy(source, target, sems.at[i])
@@ -27,7 +28,6 @@
 
     def clear(p, _):
         head[p] = -1
-        out[p] = zero
         return 0
 
     lax.fori_loop(0, places, clear, 0, unroll=8)
@@ -36,43 +36,66 @@
     live = count[0, 0]
 
     def place(s, found):
+        seconds, more = found
         p = cols[0, 0, s] * n_rows + rows[0, 0, s]
         alive = s < live
         before = head[p]
-        first = jnp.logical_and(alive, before < 0)
-        again = jnp.logical_and(alive, before >= 0)
+        vacant = before < 0
+        below = nxt[jnp.maximum(before, 0)]
+        first = jnp.logical_and(alive, vacant)
+        again = jnp.logical_and(alive, jnp.logical_not(vacant))
         head[p] = jnp.where(alive, s, before)
         nxt[s] = before
-        dups[found] = p
+        pairs[seconds] = p * slots + s
+        longer[more] = p
         pltpu.make_async_copy(
             values.at[s], out.at[jnp.where(first, p, places + s)], sem
         ).start()
-        return found + again.astype(jnp.int32)
-
-    found = lax.fori_loop(0, slots, place, 0, unroll=8)
+        second = jnp.logical_and(again, below < 0)
+        third = jnp.logical_and(again, below >= 0)
+        return seconds + second.astype(jnp.int32), more + third.astype(jnp.int32)
+
+    seconds, more = lax.fori_loop(0, slots, place, (0, 0), unroll=8)
+
+    def blank(p, _):
+        out[jnp.where(head[p] < 0, p, spare)] = zero
+        return 0
+
+    lax.fori_loop(0, places, blank, 0, unroll=8)
     pltpu.make_async_copy(values, out.at[pl.ds(places, slots)], sem).wait()
 
     def merge(i, _):
-        p = dups[i]
+        p = longer[i]
         top = head[p]
 
         @pl.when(top >= 0)
         def _():
             head[p] = -1
 
-            def more(state):
+            def going(state):
                 return nxt[state[0]] >= 0
 
             def add(state):
                 s, total = state
-                return nxt[s], total + out[places + s].astype(jnp.float32)
-
-            _, total = lax.while_loop(more, add, (top, out[p].astype(jnp.float32)))
+                tile = out[places + s].astype(jnp.float32)
+                out[places + s] = zero
+                return nxt[s], total + tile
+
+            _, total = lax.while_loop(going, add, (top, out[p].astype(jnp.float32)))
             out[p] = total.astype(jnp.bfloat16)
 
         return 0
 
-    lax.fori_loop(0, found, merge, 0)
+    lax.fori_loop(0, more, merge, 0)
+
+    def add_second(i, _):
+        p = pairs[i] // slots
+        s = pairs[i] - p * slots
+        both = out[p].astype(jnp.float32) + out[places + s].astype(jnp.float32)
+        out[p] = both.astype(jnp.bfloat16)
+        return 0
+
+    lax.fori_loop(0, seconds, add_second, 0)
 
 
 def densify(rows, cols, count, values, n_rows, n_cols):
@@ -81,7 +104,7 @@
     hbm = pl.BlockSpec(memory_space=pltpu.HBM)
     return pl.pallas_call(
         lambda *refs: densify_kernel(n_rows, *refs),
-        out_shape=pltpu.VMEM((places + slots, TILE, TILE), jnp.bfloat16),
+        out_shape=pltpu.VMEM((places + slots + 1, TILE, TILE), jnp.bfloat16),
         in_specs=[hbm, hbm, pl.BlockSpec(memory_space=pltpu.SMEM), hbm],
         out_specs=pl.BlockSpec(memory_space=pltpu.VMEM),
         scratch_shapes=[
@@ -89,6 +112,7 @@
             pltpu.SMEM(cols.shape, jnp.int32),
             pltpu.SMEM((places,), jnp.int32),
             pltpu.SMEM((slots,), jnp.int32),
+            pltpu.SMEM((slots + 1,), jnp.int32),
             pltpu.SMEM((slots + 1,), jnp.int32),
             pltpu.SemaphoreType.DMA,
             pltpu.SemaphoreType.DMA((2,)),
@@ -119,12 +143,26 @@
             device_id_type=MESH,
         )
 
+    def peer(self, d):
+        me, size = self.me, self.size
+        if self.axis == "col":
+            half = size // 2
+            step = lax.rem(1 + d, half)
+            return lax.rem(me // half + 1 - d // half, 2) * half + lax.rem(me + step, half)
+        q = self.chip(lax.div(d, 2), 1)
+        return 2 * q + lax.rem(me + 1 + d, 2)
+
+    def chip(self, d, sign):
+        q, half = self.me // 2, self.size // 4
+        step = lax.rem(1 + d, half)
+        return lax.rem(q // half + 1 - d // half, 2) * half + lax.rem(q + half + sign * step, half)
+
     def peers(self, body):
         def step(d, _):
-            body(lax.rem(self.me + d, self.size))
+            body(self.peer(d))
             return 0
 
-        lax.fori_loop(1, self.size, step, 0)
+        lax.fori_loop(0, self.size - 1, step, 0)
 
     def send(self, source, peer):
         self.copy(source, self.dst.at[self.me], peer).start()
@@ -157,6 +195,39 @@
     def receive(self, slot):
         self.copy(self.dst.at[slot], self.dst.at[slot], slot, slot).wait_recv()
 
+    def by_chip(self, source, use):
+        me, chips = self.me, self.size // 2
+        own, core = me // 2, lax.rem(me, 2)
+        beside = 2 * own + 1 - core
+
+        def send(d, _):
+            self.send(source, 2 * self.chip(d, 1) + core)
+            return 0
+
+        self.send(source, beside)
+        lax.fori_loop(0, chips - 1, send, 0)
+        self.receive(beside)
+        use(own)
+
+        def take(q):
+            slot = 2 * q + core
+            self.receive(slot)
+            self.copy(self.dst.at[slot], self.dst.at[slot], beside, slot).start()
+
+        def turn(q):
+            self.receive(2 * q + 1 - core)
+            use(q)
+
+        take(self.chip(chips - 2, -1))
+
+        def step(e, _):
+            take(self.chip(chips - 2 - e, -1))
+            turn(self.chip(chips - 1 - e, -1))
+            return 0
+
+        lax.fori_loop(1, chips - 1, step, 0)
+        turn(self.chip(0, -1))
+
 
 def rows_of(dense, i, n_rows, n_cols):
     return jnp.concatenate(
@@ -165,11 +236,11 @@
     )
 
 
-def cols_of(dense, k, n_rows):
+def cols_of(dense, q, n_rows):
     return jnp.concatenate(
         [
-            dense[pl.ds((2 * k + h) * n_rows, n_rows)].reshape(n_rows * TILE, TILE)
-            for h in range(2)
+            dense[pl.ds((4 * q + h) * n_rows, n_rows)].reshape(n_rows * TILE, TILE)
+            for h in range(4)
         ],
         axis=1,
     )
@@ -214,7 +285,6 @@
     fin,
     first_acc,
     second_acc,
-    back_acc,
     pre,
     agg,
     w2s,
@@ -222,7 +292,6 @@
     send_sems,
     x_sems,
     hw_sems,
-    grad_sems,
     recv_sems,
 ):
     n_rows, n_cols = 2 * C, 2 * R
@@ -252,7 +321,7 @@
     ex_first = Exchange("col", C, r1, send_sems.at[1], recv_sems.at[1])
     ex_hw = Gather("row", R, hw, send_sems.at[2], hw_sems)
     ex_second = Exchange("col", C, r2, send_sems.at[3], recv_sems.at[3])
-    ex_grad = Gather("col", C, gg, send_sems.at[4], grad_sems)
+    ex_grad = Exchange("col", C, gg, send_sems.at[4], recv_sems.at[4])
     ex_back = Exchange("row", R, r3, send_sems.at[5], recv_sems.at[5])
     ex_part = Exchange("col", C, r4, send_sems.at[6], recv_sems.at[6])
     ex_sum = Exchange("row", R, r5, send_sems.at[7], recv_sems.at[7])
@@ -265,51 +334,28 @@
     b2s[0:1, 0:classes] = b2[...]
     first_acc[...] = jnp.zeros_like(first_acc)
     second_acc[...] = jnp.zeros_like(second_acc)
-    back_acc[...] = jnp.zeros_like(back_acc)
     pl.semaphore_wait(barrier, R + C - 2)
 
-    core = lax.rem(row, 2)
-    beside = row + 1 - 2 * core
-
-    def send_x(d, _):
-        ex_x.send(x, lax.rem(row + 2 * d, R))
-        return 0
-
-    lax.fori_loop(1, R // 2, send_x, 0)
-    ex_x.send(x, beside)
-
-    def use_x(slot):
+    def use_x(q):
         first_acc[...] += jnp.dot(
-            cols_of(dense, slot, n_rows), xg[slot], preferred_element_type=jnp.float32
+            cols_of(dense, q, n_rows),
+            xg[pl.ds(2 * q, 2)].reshape(2 * nodes, x.shape[1]),
+            preferred_element_type=jnp.float32,
         )
 
-    use_x(row)
-    ex_x.receive(beside)
-    use_x(beside)
-
-    def pass_x(d, _):
-        slot = lax.rem(row + R - 2 * d, R)
-        ex_x.receive(slot)
-        ex_x.copy(xg.at[slot], xg.at[slot], beside, slot).start()
-        use_x(slot)
-        other = lax.rem(beside + R - 2 * d, R)
-        ex_x.receive(other)
-        use_x(other)
-        return 0
-
-    lax.fori_loop(1, R // 2, pass_x, 0)
+    ex_x.by_chip(x, use_x)
 
     def first(d, _):
-        peer = lax.rem(col + d, C)
+        peer = ex_first.peer(d)
         t1[peer] = first_acc[pl.ds(peer * nodes, nodes), :].astype(t1.dtype)
 
-        @pl.when(d < C)
+        @pl.when(d < C - 1)
         def _():
             ex_first.send(t1.at[peer], peer)
 
         return 0
 
-    lax.fori_loop(1, C + 1, first, 0)
+    lax.fori_loop(0, C, first, 0)
     r1[col] = t1[col]
     ex_first.receive_all()
 
@@ -322,33 +368,27 @@
     ).astype(jnp.bfloat16)
 
     hw[row] = s2[...]
-    ex_hw.send_all(lambda peer: s2)
-
-    def use_hw(d, _):
-        slot = lax.rem(row + R - d, R)
-
-        @pl.when(d > 0)
-        def _():
-            ex_hw.receive(slot)
-
+    def use_hw(q):
         second_acc[...] += lax.dot_general(
-            hw[slot], cols_of(dense, slot, n_rows), NT, preferred_element_type=jnp.float32
+            jnp.concatenate([hw[2 * q], hw[2 * q + 1]], axis=1),
+            cols_of(dense, q, n_rows),
+            NT,
+            preferred_element_type=jnp.float32,
         )
-        return 0
-
-    lax.fori_loop(0, R, use_hw, 0)
+
+    ex_hw.by_chip(s2, use_hw)
 
     def second(d, _):
-        peer = lax.rem(col + d, C)
+        peer = ex_second.peer(d)
         t2[peer] = second_acc[:, pl.ds(pl.multiple_of(peer * nodes, nodes), nodes)].astype(t2.dtype)
 
-        @pl.when(d < C)
+        @pl.when(d < C - 1)
         def _():
             ex_second.send(t2.at[peer], peer)
 
         return 0
 
-    lax.fori_loop(1, C + 1, second, 0)
+    lax.fori_loop(0, C, second, 0)
     r2[col] = t2[col]
     ex_second.receive_all()
 
@@ -388,31 +428,25 @@
         jnp.sum(weights, axis=1, keepdims=True), (1, TILE)
     )
 
-    def use_grad(d, _):
-        slot = lax.rem(col + C - d, C)
-
-        @pl.when(d > 0)
+    ex_grad.receive_all()
+
+    def back(d, _):
+        q = ex_back.chip(d, 1)
+        left = jnp.concatenate([gg[k] for k in range(C)], axis=1)
+        both = jnp.dot(left, cols_of(dense, q, n_rows), preferred_element_type=jnp.float32)
+        for h in range(2):
+            t3[2 * q + h] = both[:, h * nodes : (h + 1) * nodes].astype(t3.dtype)
+
+        @pl.when(d < R // 2 - 1)
         def _():
-            ex_grad.receive(slot)
-
-        back_acc[...] += jnp.dot(
-            gg[slot], rows_of(dense, slot, n_rows, n_cols), preferred_element_type=jnp.float32
-        )
+            for h in range(2):
+                ex_back.send(t3.at[2 * q + h], 2 * q + h)
+
         return 0
 
-    lax.fori_loop(0, C, use_grad, 0)
-
-    def back(d, _):
-        peer = lax.rem(row + d, R)
-        t3[peer] = back_acc[:, pl.ds(pl.multiple_of(peer * nodes, nodes), nodes)].astype(t3.dtype)
-
-        @pl.when(d < R)
-        def _():
-            ex_back.send(t3.at[peer], peer)
-
-        return 0
-
-    lax.fori_loop(1, R + 1, back, 0)
+    lax.fori_loop(0, R // 2, back, 0)
+    beside = row + 1 - 2 * lax.rem(row, 2)
+    ex_back.send(t3.at[beside], beside)
     r3[row] = t3[row]
     ex_back.receive_all()
 
@@ -555,7 +589,6 @@
         pltpu.VMEM((C, piece, TILE), bf16),
         pltpu.VMEM((C * nodes, features), f32),
         pltpu.VMEM((PADDED, C * nodes), f32),
-        pltpu.VMEM((PADDED, R * nodes), f32),
         pltpu.VMEM((nodes, hidden), f32),
         pltpu.VMEM((nodes, features), bf16),
         pltpu.VMEM((PADDED, hidden), f32),
@@ -563,7 +596,6 @@
         pltpu.SemaphoreType.DMA((9,)),
         pltpu.SemaphoreType.DMA((R,)),
         pltpu.SemaphoreType.DMA((R,)),
-        pltpu.SemaphoreType.DMA((C,)),
         pltpu.SemaphoreType.DMA((9,)),
     ]
     hidden_now, logits_now, sums = pl.pallas_call(

time: 91 us -> 85.7 us (0.942)
  Pallas kernels: 89.3 us -> 84.1 us
    pallas_call x1, Pallas kernels: 80.7 us -> 74.1 us  [on_device(): pl.pallas_call(lambda *refs: step_kernel(R, C, *refs), out_shape=(pltpu.V...]
    pallas_call x1, Pallas kernels: 7.26 us -> 8.59 us  [densify(): pl.pallas_call(lambda *refs: densify_kernel(n_rows, *refs), out_shape=plt...]
where the time goes in v4:
time: 85.7 us; the launch traced here: 85.5 us
  Pallas kernels  84.1 us (98%)
  between operations  1.46 us (2%)
    pallas_call x1, Pallas kernels, on_device(): pl.pallas_call(lambda *refs: step_kernel(R, C, *refs), out_shape=(pltpu.V...  74.1 us
    pallas_call x1, Pallas kernels, densify(): pl.pallas_call(lambda *refs: densify_kernel(n_rows, *refs), out_shape=plt...  8.59 us

profile of v4, /device:TPU:1, one launch (start us, length us, event | category | flops | bytes accessed | tf_op | source)
XLA Modules:
  0.0 85.5 jit_solution(1842212783885006379)
XLA Ops:
  0.6 0.0 copy-start.6
  0.6 0.0 copy-start.2
  0.7 0.0 copy-start.5
  0.7 0.0 copy-start.1
  0.7 0.0 copy-start.4
  0.7 0.0 copy-start.3
  0.7 0.0 copy-start
  1.4 8.6 %densify.1.refs_1_ = bf16[897,128,128]{2,1,0:T(8,128)(2,1)S(1)} custom-call(s32[1,1,384]{2,1,0:T(1,128)} %refs_0_.2, s32[1,1,384]{2,1,0:T(1,128)} %refs_1_.1, s32[1,1]{1,0:T(1,128)S(6)} %copy.18.refs_2_, bf16[384,128,128]{2,1,0:T(8,128)(2,1)} %bitcast.15), custom_call_target="tpu_custom_call" | custom-call | tf_op jit(solution)/shard_map/densify/pallas_call | solution.py:105
  10.0 0.0 copy-done.6
  10.0 0.0 copy-done.2
  10.0 0.0 copy-done.5
  10.0 0.0 copy-done.1
  10.0 0.0 copy-done.4
  10.1 0.0 copy-done.3
  10.1 0.0 copy-done
  10.1 74.1 %step.1 = (bf16[256,256]{1,0:T(8,128)(2,1)S(1)}, f32[47,256]{1,0:T(8,128)S(1)}, f32[384,128]{1,0:T(8,128)S(1)}) custom-call(bf16[256,128]{1,0:T(8,128)(2,1)S(1)} %copy-done, bf16[897,128,128]{2,1,0:T(8,128)(2,1)S(1)} %densify.1.refs_1_, s32[1,256]{1,0:T(1,128)S(1)} %bitcast.11, s32[1,256]{1,0:T(1,128)S(1)} %bitcast.12, bf16[128,256]{1,0:T(8,128)(2,1)S(1)} %copy-done.1, ...), custom_call_target="tpu_custom_call" | custom-call | tf_op jit(solution)/shard_map/step/pallas_call | solution.py:601
  84.2 1.3 %finish.1 = (bf16[256,256]{1,0:T(8,128)(2,1)}, f32[47,256]{1,0:T(8,128)}, f32[1,1]{1,0:T(1,128)}, f32[128,256]{1,0:T(8,128)}, f32[1,256]{1,0:T(1,128)}, /*index=5*/f32[47,256]{1,0:T(8,128)}, f32[1,47]{1,0:T(1,128)}) custom-call(bf16[256,256]{1,0:T(8,128)(2,1)S(1)} %get-tuple-element.17.refs_0_, f32[47,256]{1,0:T(8,128)S(1)} %get-tuple-element.18.refs_1_, ...), custom_call_target="tpu_custom_call" | custom-call | tf_op jit(solution)/shard_map/finish/pallas_call | solution.py:625
Async XLA Ops:
  0.6 9.4 %copy-start.6 = (f32[47]{0:T(128)S(1)}, f32[47]{0:T(128)}, u32[]{:S(2)}) copy-start(f32[47]{0:T(128)} %param.21) | copy-start | bytes 568
  0.6 9.4 %copy-start.2 = (bf16[256,47]{0,1:T(8,128)(2,1)S(1)}, bf16[256,47]{0,1:T(8,128)(2,1)}, u32[]{:S(2)}) copy-start(bf16[256,47]{0,1:T(8,128)(2,1)} %param.20) | copy-start | bytes 72196
  0.7 9.4 %copy-start.5 = (f32[256]{0:T(256)S(1)}, f32[256]{0:T(256)}, u32[]{:S(2)}) copy-start(f32[256]{0:T(256)} %param.19) | copy-start | bytes 3076
  0.7 9.4 %copy-start.1 = (bf16[128,256]{1,0:T(8,128)(2,1)S(1)}, bf16[128,256]{1,0:T(8,128)(2,1)}, u32[]{:S(2)}) copy-start(bf16[128,256]{1,0:T(8,128)(2,1)} %refs_4_.1) | copy-start | bytes 196612
  0.7 9.4 %copy-start.4 = (s32[256]{0:T(256)S(1)}, s32[256]{0:T(256)}, u32[]{:S(2)}) copy-start(s32[256]{0:T(256)} %param.17) | copy-start | bytes 3076
  0.7 9.4 %copy-start.3 = (s32[256]{0:T(256)S(1)}, s32[256]{0:T(256)}, u32[]{:S(2)}) copy-start(s32[256]{0:T(256)} %param.16) | copy-start | bytes 3076
  0.7 9.4 %copy-start = (bf16[256,128]{1,0:T(8,128)(2,1)S(1)}, bf16[256,128]{1,0:T(8,128)(2,1)}, u32[]{:S(2)}) copy-start(bf16[256,128]{1,0:T(8,128)(2,1)} %refs_0_.3) | copy-start | bytes 196612

commit v5 on v4

--- a/solution.py
+++ b/solution.py
@@ -16,6 +16,7 @@
     slots = values.shape[0]
     places = head.shape[0]
     spare = places + slots
+    several = 1 << (slots - 1).bit_length()
     zero = jnp.zeros((TILE, TILE), jnp.bfloat16)
     loads = [
         pltpu.make_async_copy(source, target, sems.at[i])
@@ -41,21 +42,23 @@
         alive = s < live
         before = head[p]
         vacant = before < 0
-        below = nxt[jnp.maximum(before, 0)]
-        first = jnp.logical_and(alive, vacant)
-        again = jnp.logical_and(alive, jnp.logical_not(vacant))
-        head[p] = jnp.where(alive, s, before)
+        head[p] = jnp.where(alive, jnp.where(vacant, s, s + several), before)
         nxt[s] = before
-        pairs[seconds] = p * slots + s
+        pairs[seconds] = p * several + s
         longer[more] = p
         pltpu.make_async_copy(
-            values.at[s], out.at[jnp.where(first, p, places + s)], sem
+            values.at[s],
+            out.at[jnp.where(jnp.logical_and(alive, vacant), p, places + s)],
+            sem,
         ).start()
-        second = jnp.logical_and(again, below < 0)
-        third = jnp.logical_and(again, below >= 0)
+        third = jnp.logical_and(alive, before >= several)
+        second = jnp.logical_and(alive, jnp.logical_and(before >= 0, before < several))
         return seconds + second.astype(jnp.int32), more + third.astype(jnp.int32)
 
     seconds, more = lax.fori_loop(0, slots, place, (0, 0), unroll=8)
+
+    def slot_of(entry):
+        return jnp.where(entry >= several, entry - several, entry)
 
     def blank(p, _):
         out[jnp.where(head[p] < 0, p, spare)] = zero
@@ -66,7 +69,7 @@
 
     def merge(i, _):
         p = longer[i]
-        top = head[p]
+        top = slot_of(head[p])
 
         @pl.when(top >= 0)
         def _():
@@ -79,7 +82,7 @@
                 s, total = state
                 tile = out[places + s].astype(jnp.float32)
                 out[places + s] = zero
-                return nxt[s], total + tile
+                return slot_of(nxt[s]), total + tile
 
             _, total = lax.while_loop(going, add, (top, out[p].astype(jnp.float32)))
             out[p] = total.astype(jnp.bfloat16)
@@ -89,8 +92,8 @@
     lax.fori_loop(0, more, merge, 0)
 
     def add_second(i, _):
-        p = pairs[i] // slots
-        s = pairs[i] - p * slots
+        p = pairs[i] // several
+        s = pairs[i] - p * several
         both = out[p].astype(jnp.float32) + out[places + s].astype(jnp.float32)
         out[p] = both.astype(jnp.bfloat16)
         return 0
@@ -197,41 +200,49 @@
 
     def by_chip(self, source, use):
         me, chips = self.me, self.size // 2
-        own, core = me // 2, lax.rem(me, 2)
+        own, core, half = me // 2, lax.rem(me, 2), self.size // 4
         beside = 2 * own + 1 - core
 
-        def send(d, _):
-            self.send(source, 2 * self.chip(d, 1) + core)
+        def send(e, _):
+            self.send(source, 2 * self.chip(chips - 2 - e, 1) + core)
             return 0
-
-        self.send(source, beside)
-        lax.fori_loop(0, chips - 1, send, 0)
-        self.receive(beside)
-        use(own)
 
         def take(q):
             slot = 2 * q + core
             self.receive(slot)
             self.copy(self.dst.at[slot], self.dst.at[slot], beside, slot).start()
 
-        def turn(q):
-            self.receive(2 * q + 1 - core)
-            use(q)
-
-        take(self.chip(chips - 2, -1))
-
-        def step(e, _):
+        def near(e, _):
             take(self.chip(chips - 2 - e, -1))
-            turn(self.chip(chips - 1 - e, -1))
             return 0
 
-        lax.fori_loop(1, chips - 1, step, 0)
-        turn(self.chip(0, -1))
-
-
-def rows_of(dense, i, n_rows, n_cols):
+        def near_other(e, _):
+            self.receive(2 * self.chip(chips - 1 - e, -1) + 1 - core)
+            return 0
+
+        def far(e, _):
+            take(self.chip(half - 1 - e, -1))
+            use(self.chip(chips - 1 - e, -1))
+            return 0
+
+        def far_other(e, _):
+            self.receive(2 * self.chip(half - 1 - e, -1) + 1 - core)
+            return 0
+
+        self.send(source, beside)
+        lax.fori_loop(0, chips - 1, send, 0)
+        lax.fori_loop(0, half - 1, near, 0)
+        lax.fori_loop(0, half, near_other, 0)
+        lax.fori_loop(0, half, far, 0)
+        lax.fori_loop(0, half, far_other, 0)
+
+
+def rows_of(dense, i, start, n_rows, n_cols):
     return jnp.concatenate(
-        [dense[pl.ds(k * n_rows + 2 * i, 2)].reshape(2 * TILE, TILE) for k in range(n_cols)],
+        [
+            dense[pl.ds((start + k) * n_rows + 2 * i, 2)].reshape(2 * TILE, TILE)
+            for k in range(n_cols)
+        ],
         axis=1,
     )
 
@@ -344,10 +355,16 @@
         )
 
     ex_x.by_chip(x, use_x)
+    far = (R // 2) * (1 - row // (R // 2))
 
     def first(d, _):
         peer = ex_first.peer(d)
-        t1[peer] = first_acc[pl.ds(peer * nodes, nodes), :].astype(t1.dtype)
+        rest = jnp.dot(
+            rows_of(dense, peer, 2 * far, n_rows, R),
+            xg[pl.ds(far, R // 2)].reshape(R // 2 * nodes, x.shape[1]),
+            preferred_element_type=jnp.float32,
+        )
+        t1[peer] = (first_acc[pl.ds(peer * nodes, nodes), :] + rest).astype(t1.dtype)
 
         @pl.when(d < C - 1)
         def _():
@@ -380,7 +397,14 @@
 
     def second(d, _):
         peer = ex_second.peer(d)
-        t2[peer] = second_acc[:, pl.ds(pl.multiple_of(peer * nodes, nodes), nodes)].astype(t2.dtype)
+        rest = lax.dot_general(
+            jnp.concatenate([hw[far + k] for k in range(R // 2)], axis=1),
+            rows_of(dense, peer, 2 * far, n_rows, R),
+            NT,
+            preferred_element_type=jnp.float32,
+        )
+        near = second_acc[:, pl.ds(pl.multiple_of(peer * nodes, nodes), nodes)]
+        t2[peer] = (near + rest).astype(t2.dtype)
 
         @pl.when(d < C - 1)
         def _():

time: 85.7 us -> 83.1 us (0.970)
  Pallas kernels: 84.1 us -> 81.1 us
    pallas_call x1, Pallas kernels: 74.1 us -> 71.5 us  [on_device(): pl.pallas_call(lambda *refs: step_kernel(R, C, *refs), out_shape=(pltpu.V...]
where the time goes in v5:
time: 83.1 us; the launch traced here: 82.6 us
  Pallas kernels  81.1 us (98%)
  between operations  1.46 us (2%)
    pallas_call x1, Pallas kernels, on_device(): pl.pallas_call(lambda *refs: step_kernel(R, C, *refs), out_shape=(pltpu.V...  71.5 us
    pallas_call x1, Pallas kernels, densify(): pl.pallas_call(lambda *refs: densify_kernel(n_rows, *refs), out_shape=plt...  8.3 us

profile of v5, /device:TPU:1, one launch (start us, length us, event | category | flops | bytes accessed | tf_op | source)
XLA Modules:
  0.0 82.6 jit_solution(11061529270388245873)
XLA Ops:
  0.6 0.0 copy-start.6
  0.6 0.0 copy-start.2
  0.7 0.0 copy-start.5
  0.7 0.0 copy-start.1
  0.7 0.0 copy-start.4
  0.7 0.0 copy-start.3
  0.7 0.0 copy-start
  1.4 8.3 %densify.1.refs_1_ = bf16[897,128,128]{2,1,0:T(8,128)(2,1)S(1)} custom-call(s32[1,1,384]{2,1,0:T(1,128)} %refs_0_.2, s32[1,1,384]{2,1,0:T(1,128)} %refs_1_.1, s32[1,1]{1,0:T(1,128)S(6)} %copy.18.refs_2_, bf16[384,128,128]{2,1,0:T(8,128)(2,1)} %bitcast.15), custom_call_target="tpu_custom_call" | custom-call | tf_op jit(solution)/shard_map/densify/pallas_call | solution.py:108
  9.7 0.0 copy-done.6
  9.7 0.0 copy-done.2
  9.7 0.0 copy-done.5
  9.7 0.0 copy-done.1
  9.8 0.0 copy-done.4
  9.8 0.0 copy-done.3
  9.8 0.0 copy-done
  9.8 71.5 %step.1 = (bf16[256,256]{1,0:T(8,128)(2,1)S(1)}, f32[47,256]{1,0:T(8,128)S(1)}, f32[384,128]{1,0:T(8,128)S(1)}) custom-call(bf16[256,128]{1,0:T(8,128)(2,1)S(1)} %copy-done, bf16[897,128,128]{2,1,0:T(8,128)(2,1)S(1)} %densify.1.refs_1_, s32[1,256]{1,0:T(1,128)S(1)} %bitcast.11, s32[1,256]{1,0:T(1,128)S(1)} %bitcast.12, bf16[128,256]{1,0:T(8,128)(2,1)S(1)} %copy-done.1, ...), custom_call_target="tpu_custom_call" | custom-call | tf_op jit(solution)/shard_map/step/pallas_call | solution.py:625
  81.3 1.3 %finish.1 = (bf16[256,256]{1,0:T(8,128)(2,1)}, f32[47,256]{1,0:T(8,128)}, f32[1,1]{1,0:T(1,128)}, f32[128,256]{1,0:T(8,128)}, f32[1,256]{1,0:T(1,128)}, /*index=5*/f32[47,256]{1,0:T(8,128)}, f32[1,47]{1,0:T(1,128)}) custom-call(bf16[256,256]{1,0:T(8,128)(2,1)S(1)} %get-tuple-element.17.refs_0_, f32[47,256]{1,0:T(8,128)S(1)} %get-tuple-element.18.refs_1_, ...), custom_call_target="tpu_custom_call" | custom-call | tf_op jit(solution)/shard_map/finish/pallas_call | solution.py:649
Async XLA Ops:
  0.6 9.1 %copy-start.6 = (f32[47]{0:T(128)S(1)}, f32[47]{0:T(128)}, u32[]{:S(2)}) copy-start(f32[47]{0:T(128)} %param.21) | copy-start | bytes 568
  0.6 9.1 %copy-start.2 = (bf16[256,47]{0,1:T(8,128)(2,1)S(1)}, bf16[256,47]{0,1:T(8,128)(2,1)}, u32[]{:S(2)}) copy-start(bf16[256,47]{0,1:T(8,128)(2,1)} %param.20) | copy-start | bytes 72196
  0.7 9.1 %copy-start.5 = (f32[256]{0:T(256)S(1)}, f32[256]{0:T(256)}, u32[]{:S(2)}) copy-start(f32[256]{0:T(256)} %param.19) | copy-start | bytes 3076
  0.7 9.1 %copy-start.1 = (bf16[128,256]{1,0:T(8,128)(2,1)S(1)}, bf16[128,256]{1,0:T(8,128)(2,1)}, u32[]{:S(2)}) copy-start(bf16[128,256]{1,0:T(8,128)(2,1)} %refs_4_.1) | copy-start | bytes 196612
  0.7 9.1 %copy-start.4 = (s32[256]{0:T(256)S(1)}, s32[256]{0:T(256)}, u32[]{:S(2)}) copy-start(s32[256]{0:T(256)} %param.17) | copy-start | bytes 3076
  0.7 9.1 %copy-start.3 = (s32[256]{0:T(256)S(1)}, s32[256]{0:T(256)}, u32[]{:S(2)}) copy-start(s32[256]{0:T(256)} %param.16) | copy-start | bytes 3076
  0.7 9.1 %copy-start = (bf16[256,128]{1,0:T(8,128)(2,1)S(1)}, bf16[256,128]{1,0:T(8,128)(2,1)}, u32[]{:S(2)}) copy-start(bf16[256,128]{1,0:T(8,128)(2,1)} %refs_0_.3) | copy-start | bytes 196612

commit v6 on v5

--- a/solution.py
+++ b/solution.py
@@ -15,7 +15,6 @@
 def densify_kernel(n_rows, rows_in, cols_in, count, values, out, rows, cols, head, nxt, pairs, longer, sem, sems):
     slots = values.shape[0]
     places = head.shape[0]
-    spare = places + slots
     several = 1 << (slots - 1).bit_length()
     zero = jnp.zeros((TILE, TILE), jnp.bfloat16)
     loads = [
@@ -29,6 +28,7 @@
 
     def clear(p, _):
         head[p] = -1
+        out[p] = zero
         return 0
 
     lax.fori_loop(0, places, clear, 0, unroll=8)
@@ -60,11 +60,6 @@
     def slot_of(entry):
         return jnp.where(entry >= several, entry - several, entry)
 
-    def blank(p, _):
-        out[jnp.where(head[p] < 0, p, spare)] = zero
-        return 0
-
-    lax.fori_loop(0, places, blank, 0, unroll=8)
     pltpu.make_async_copy(values, out.at[pl.ds(places, slots)], sem).wait()
 
     def merge(i, _):
@@ -92,13 +87,20 @@
     lax.fori_loop(0, more, merge, 0)
 
     def add_second(i, _):
-        p = pairs[i] // several
-        s = pairs[i] - p * several
-        both = out[p].astype(jnp.float32) + out[places + s].astype(jnp.float32)
-        out[p] = both.astype(jnp.bfloat16)
+        sums = []
+        for j in range(2):
+            entry = jnp.where(2 * i + j < seconds, pairs[2 * i + j], places * several + slots)
+            p = entry // several
+            s = entry - p * several
+            p = jnp.where(p == places, places + slots, p)
+            total = out[p].astype(jnp.float32) + out[places + s].astype(jnp.float32)
+            sums.append((p, total.astype(jnp.bfloat16)))
+        for p, total in sums:
+            out[p] = total
         return 0
 
-    lax.fori_loop(0, seconds, add_second, 0)
+    out[places + slots] = zero
+    lax.fori_loop(0, (seconds + 1) // 2, add_second, 0)
 
 
 def densify(rows, cols, count, values, n_rows, n_cols):
@@ -115,7 +117,7 @@
             pltpu.SMEM(cols.shape, jnp.int32),
             pltpu.SMEM((places,), jnp.int32),
             pltpu.SMEM((slots,), jnp.int32),
-            pltpu.SMEM((slots + 1,), jnp.int32),
+            pltpu.SMEM((slots + 2,), jnp.int32),
             pltpu.SMEM((slots + 1,), jnp.int32),
             pltpu.SemaphoreType.DMA,
             pltpu.SemaphoreType.DMA((2,)),
@@ -235,6 +237,29 @@
         lax.fori_loop(0, half, near_other, 0)
         lax.fori_loop(0, half, far, 0)
         lax.fori_loop(0, half, far_other, 0)
+
+    def direct(self, source, use):
+        core, chips, half = lax.rem(self.me, 2), self.size // 2, self.size // 4
+
+        def both(q):
+            self.receive(2 * q)
+            self.receive(2 * q + 1)
+
+        def near(e, _):
+            q = self.chip(chips - 1 - e, -1)
+            both(q)
+            use(q)
+            return 0
+
+        def far(e, _):
+            both(self.chip(half - 1 - e, -1))
+            return 0
+
+        self.send_all(lambda peer: source)
+        self.receive(2 * (self.me // 2) + 1 - core)
+        use(self.me // 2)
+        lax.fori_loop(1, half, near, 0)
+        lax.fori_loop(0, half, far, 0)
 
 
 def rows_of(dense, i, start, n_rows, n_cols):
@@ -393,7 +418,7 @@
             preferred_element_type=jnp.float32,
         )
 
-    ex_hw.by_chip(s2, use_hw)
+    ex_hw.direct(s2, use_hw)
 
     def second(d, _):
         peer = ex_second.peer(d)

time: 83.1 us -> 82.1 us (0.988)
  Pallas kernels: 81.1 us -> 80.2 us
    pallas_call x1, Pallas kernels: 71.5 us -> 70.5 us  [on_device(): pl.pallas_call(lambda *refs: step_kernel(R, C, *refs), out_shape=(pltpu.V...]
where the time goes in v6:
time: 82.1 us; the launch traced here: 81.6 us
  Pallas kernels  80.2 us (98%)
  between operations  1.46 us (2%)
    pallas_call x1, Pallas kernels, on_device(): pl.pallas_call(lambda *refs: step_kernel(R, C, *refs), out_shape=(pltpu.V...  70.5 us
    pallas_call x1, Pallas kernels, densify(): pl.pallas_call(lambda *refs: densify_kernel(n_rows, *refs), out_shape=plt...  8.31 us

profile of v6, /device:TPU:1, one launch (start us, length us, event | category | flops | bytes accessed | tf_op | source)
XLA Modules:
  0.0 81.6 jit_solution(4590960237536649986)
XLA Ops:
  0.6 0.0 copy-start.6
  0.6 0.0 copy-start.2
  0.7 0.0 copy-start.5
  0.7 0.0 copy-start.1
  0.7 0.0 copy-start.4
  0.7 0.0 copy-start.3
  0.7 0.0 copy-start
  1.4 8.3 %densify.1.refs_1_ = bf16[897,128,128]{2,1,0:T(8,128)(2,1)S(1)} custom-call(s32[1,1,384]{2,1,0:T(1,128)} %refs_0_.2, s32[1,1,384]{2,1,0:T(1,128)} %refs_1_.1, s32[1,1]{1,0:T(1,128)S(6)} %copy.18.refs_2_, bf16[384,128,128]{2,1,0:T(8,128)(2,1)} %bitcast.15), custom_call_target="tpu_custom_call" | custom-call | tf_op jit(solution)/shard_map/densify/pallas_call | solution.py:110
  9.7 0.0 copy-done.6
  9.7 0.0 copy-done.2
  9.7 0.0 copy-done.5
  9.8 0.0 copy-done.1
  9.8 0.0 copy-done.4
  9.8 0.0 copy-done.3
  9.8 0.0 copy-done
  9.8 70.5 %step.1 = (bf16[256,256]{1,0:T(8,128)(2,1)S(1)}, f32[47,256]{1,0:T(8,128)S(1)}, f32[384,128]{1,0:T(8,128)S(1)}) custom-call(bf16[256,128]{1,0:T(8,128)(2,1)S(1)} %copy-done, bf16[897,128,128]{2,1,0:T(8,128)(2,1)S(1)} %densify.1.refs_1_, s32[1,256]{1,0:T(1,128)S(1)} %bitcast.11, s32[1,256]{1,0:T(1,128)S(1)} %bitcast.12, bf16[128,256]{1,0:T(8,128)(2,1)S(1)} %copy-done.1, ...), custom_call_target="tpu_custom_call" | custom-call | tf_op jit(solution)/shard_map/step/pallas_call | solution.py:650
  80.3 1.3 %finish.1 = (bf16[256,256]{1,0:T(8,128)(2,1)}, f32[47,256]{1,0:T(8,128)}, f32[1,1]{1,0:T(1,128)}, f32[128,256]{1,0:T(8,128)}, f32[1,256]{1,0:T(1,128)}, /*index=5*/f32[47,256]{1,0:T(8,128)}, f32[1,47]{1,0:T(1,128)}) custom-call(bf16[256,256]{1,0:T(8,128)(2,1)S(1)} %get-tuple-element.17.refs_0_, f32[47,256]{1,0:T(8,128)S(1)} %get-tuple-element.18.refs_1_, ...), custom_call_target="tpu_custom_call" | custom-call | tf_op jit(solution)/shard_map/finish/pallas_call | solution.py:674
Async XLA Ops:
  0.6 9.1 %copy-start.6 = (f32[47]{0:T(128)S(1)}, f32[47]{0:T(128)}, u32[]{:S(2)}) copy-start(f32[47]{0:T(128)} %param.21) | copy-start | bytes 568
  0.6 9.1 %copy-start.2 = (bf16[256,47]{0,1:T(8,128)(2,1)S(1)}, bf16[256,47]{0,1:T(8,128)(2,1)}, u32[]{:S(2)}) copy-start(bf16[256,47]{0,1:T(8,128)(2,1)} %param.20) | copy-start | bytes 72196
  0.7 9.1 %copy-start.5 = (f32[256]{0:T(256)S(1)}, f32[256]{0:T(256)}, u32[]{:S(2)}) copy-start(f32[256]{0:T(256)} %param.19) | copy-start | bytes 3076
  0.7 9.1 %copy-start.1 = (bf16[128,256]{1,0:T(8,128)(2,1)S(1)}, bf16[128,256]{1,0:T(8,128)(2,1)}, u32[]{:S(2)}) copy-start(bf16[128,256]{1,0:T(8,128)(2,1)} %refs_4_.1) | copy-start | bytes 196612
  0.7 9.1 %copy-start.4 = (s32[256]{0:T(256)S(1)}, s32[256]{0:T(256)}, u32[]{:S(2)}) copy-start(s32[256]{0:T(256)} %param.17) | copy-start | bytes 3076
  0.7 9.1 %copy-start.3 = (s32[256]{0:T(256)S(1)}, s32[256]{0:T(256)}, u32[]{:S(2)}) copy-start(s32[256]{0:T(256)} %param.16) | copy-start | bytes 3076
  0.7 9.1 %copy-start = (bf16[256,128]{1,0:T(8,128)(2,1)S(1)}, bf16[256,128]{1,0:T(8,128)(2,1)}, u32[]{:S(2)}) copy-start(bf16[256,128]{1,0:T(8,128)(2,1)} %refs_0_.3) | copy-start | bytes 196612
